TPU v7x, 256 devices: a whole 4x4x8 slice. The times are simulated.
256 devices in a mesh: dp: 32 (over z, y), mp: 8 (over x, core).
Axes of the slice: x: 4, y: 4, z: 8, core: 2. Of those that a mesh axis runs over, the one named last changes fastest.
Arguments:
- enc_context: bfloat16 [4096, 2048], P('dp', 'mp'), may hold values from -6 to 6
- enc_resid: bfloat16 [4096, 4096], P('dp', 'mp'), may hold values from -8 to 8
- enc_out_w: bfloat16 [2048, 4096], P('mp'), may hold values from -0.25 to 0.25
- final_gain: bfloat16 [4096], P('mp'), may hold values from 0.099609375 to 1.8984375
- kv_weight: bfloat16 [2, 4096, 2048], P(None, None, 'mp'), may hold values from -0.09375 to 0.09375
- img_queries: bfloat16 [4096, 2048], P('dp', 'mp'), may hold values from -48 to 48
- img_resid: bfloat16 [4096, 4096], P('dp', 'mp'), may hold values from -8 to 8
- dec_out_w: bfloat16 [2048, 4096], P('mp'), may hold values from -0.25 to 0.25
- moe_gain: bfloat16 [4096], P('mp'), may hold values from 0.099609375 to 1.8984375
- router_w: bfloat16 [4096, 32], P('mp'), may hold values from -0.1875 to 0.1875
- expert_ids: int32 [4096, 2], P('dp'), may hold values from 0 to 31, all different within a row; in each aligned block of 128 rows (0 to 127, 128 to 255, ...) at most 24 rows name the same one
- text_lengths: int32 [32], P('dp'), may hold values from 1 to 128, 2560 in all
- expert_in: bfloat16 [32, 4096, 2048], P('dp', None, 'mp'), may hold values from -0.09375 to 0.09375
- expert_out: bfloat16 [32, 2048, 4096], P('dp', 'mp'), may hold values from -0.1875 to 0.1875
Outputs:
- encoded: bfloat16 [4096, 4096], P('dp', 'mp')
- mixed: bfloat16 [4096, 4096], P('dp', 'mp')
Inputs may be any that keep to these rules, and one draw needn't show every extreme that they name: `expert_ids`: the two experts of a row differ. Within each aligned block of 128 rows (one sample) no expert is named by more than 24 rows, a bound that some block of every draw reaches.
All inputs are finite; a program needn't handle non-finite values. No bound on the sum of `text_lengths` on one device may be relied on, other than what follows from the above.
Results may differ from a plain program's by a relative error of at most 0.013.
Values may be sent and summed in bfloat16 or wider, within the bound.
A program may use at most 128 MiB of HBM per device.

v0:
```python
import jax
import jax.numpy as jnp
from jax import lax
from jax.sharding import PartitionSpec as P

HD = 64


EPSILON = 1e-06
SCORE_SCALE = 0.125


def slot_table(expert_ids, expert_count):
    pair_ids = expert_ids.reshape(-1)
    onehot = (pair_ids[:, None] == jnp.arange(expert_count, dtype=jnp.int32)[None, :]).astype(
        jnp.int32
    )
    earlier = jnp.cumsum(onehot, axis=0) - onehot
    return jnp.sum(earlier * onehot, axis=1)


def local(
    enc_context,
    enc_resid,
    enc_out_w,
    final_gain,
    kv_weight,
    img_queries,
    img_resid,
    dec_out_w,
    moe_gain,
    router_w,
    expert_ids,
    text_lengths,
    expert_in,
    expert_out,
):
    full_width = enc_out_w.shape[1]
    text_part = jnp.dot(enc_context, enc_out_w, preferred_element_type=jnp.float32)
    text_state = enc_resid.astype(jnp.float32) + lax.psum_scatter(
        text_part, "mp", scatter_dimension=1, tiled=True
    )
    text_square = lax.psum(jnp.sum(text_state * text_state, axis=1), "mp")
    text_scale = lax.rsqrt(text_square / full_width + EPSILON)
    encoded = (text_state * final_gain.astype(jnp.float32) * text_scale[:, None]).astype(
        jnp.bfloat16
    )
    heads_width = kv_weight.shape[2]
    text_count = encoded.shape[0]
    kv_sums = jnp.einsum(
        "tf,cfh->cth",
        lax.all_gather(encoded, "mp", axis=1, tiled=True),
        kv_weight,
        preferred_element_type=jnp.float32,
    )
    key_rows = kv_sums[0].astype(jnp.bfloat16)
    value_rows = kv_sums[1].astype(jnp.bfloat16)
    row_count = img_queries.shape[0]
    head_count = heads_width // HD
    query_heads = img_queries.reshape(row_count, head_count, HD)
    key_heads = key_rows.reshape(text_count, head_count, HD)
    value_heads = value_rows.reshape(text_count, head_count, HD)
    scores = (
        jnp.einsum("qhd,khd->hqk", query_heads, key_heads, preferred_element_type=jnp.float32)
        * SCORE_SCALE
    )
    valid = jnp.arange(text_count, dtype=jnp.int32)[None, None, :] < text_lengths[0]
    scores = jnp.where(valid, scores, -jnp.inf)
    probs = jax.nn.softmax(scores, axis=-1).astype(jnp.bfloat16)
    context = jnp.einsum("hqk,khd->qhd", probs, value_heads, preferred_element_type=jnp.float32)
    context = context.reshape(row_count, heads_width).astype(jnp.bfloat16)
    cross_part = jnp.dot(context, dec_out_w, preferred_element_type=jnp.float32)
    hidden = img_resid.astype(jnp.float32) + lax.psum_scatter(
        cross_part, "mp", scatter_dimension=1, tiled=True
    )
    gained = hidden * moe_gain.astype(jnp.float32)
    router_slice = router_w.astype(jnp.float32)
    square_sum = lax.psum(jnp.sum(hidden * hidden, axis=1), "mp")
    rms_scale = lax.rsqrt(square_sum / full_width + EPSILON)
    logits = lax.psum(
        jnp.dot(gained * rms_scale[:, None], router_slice, precision=lax.Precision.HIGHEST), "mp"
    )
    normed = (gained * rms_scale[:, None]).astype(jnp.bfloat16)
    expert_count = router_w.shape[1]
    choose = (
        expert_ids[:, :, None] == jnp.arange(expert_count, dtype=jnp.int32)[None, None, :]
    ).astype(jnp.float32)
    picked = jnp.sum(choose * logits[:, None, :], axis=2)
    gates = jax.nn.softmax(picked, axis=1)
    capacity = 3 * row_count * 2 // expert_count
    flat_ids = expert_ids.reshape(-1)
    flat_slots = slot_table(expert_ids, expert_count)
    full_rows = lax.all_gather(normed, "mp", axis=1, tiled=True)
    packed = (
        jnp.zeros((expert_count, capacity, full_width), jnp.bfloat16)
        .at[flat_ids, flat_slots]
        .set(jnp.repeat(full_rows, 2, axis=0))
    )
    arrived = lax.all_to_all(packed, "dp", split_axis=0, concat_axis=0, tiled=True)
    source_count = arrived.shape[0]
    flat_in = arrived.reshape(source_count * capacity, full_width)
    inner = jax.nn.gelu(
        jnp.dot(flat_in, expert_in[0], preferred_element_type=jnp.float32), approximate=True
    ).astype(jnp.bfloat16)
    result = jnp.dot(inner, expert_out[0], preferred_element_type=jnp.float32).reshape(
        source_count, capacity, full_width
    )
    returned = lax.all_to_all(result, "dp", split_axis=0, concat_axis=0, tiled=True)
    fetched = returned[flat_ids, flat_slots].reshape(row_count, 2, full_width)
    moe_part = jnp.sum(fetched * gates[:, :, None], axis=1)
    moe = lax.psum_scatter(moe_part, "mp", scatter_dimension=1, tiled=True)
    mixed = (hidden + moe).astype(jnp.bfloat16)
    return (encoded, mixed)


def solution(mesh):
    placed = (
        P("dp", "mp"),
        P("dp", "mp"),
        P("mp", None),
        P("mp"),
        P(None, None, "mp"),
        P("dp", "mp"),
        P("dp", "mp"),
        P("mp", None),
        P("mp"),
        P("mp", None),
        P("dp", None),
        P("dp"),
        P("dp", None, "mp"),
        P("dp", "mp", None),
    )
    return jax.shard_map(
        local, mesh=mesh, in_specs=placed, out_specs=(P("dp", "mp"), P("dp", "mp")), check_vma=False
    )
```

profile of v0, /device:TPU:1, one launch (start us, length us, event | category | flops | bytes accessed | tf_op | source)
XLA Modules:
  0.0 779.1 jit_solution(14209533508000615425)
XLA Ops:
  7.2 3.6 fusion.40
  11.5 37.0 %reduce-scatter.4.cloned.1.call-done = f32[128,512]{1,0:T(8,128)} async-done(((f32[128,4096]{1,0:T(8,128)}), f32[128,512]{1,0:T(8,128)}) %reduce-scatter.4.cloned.1.call-update) | async-done | bytes 262160 | tf_op jit(solution)/shard_map/reduce_scatter | solution.py:40
  49.5 15.0 %psum.21 = f32[128]{0:T(128)S(1)} all-reduce(f32[128]{0:T(128)S(1)} %multiply_reduce_fusion.2), channel_id=1, replica_groups=mesh['dp'=32,'mp'=8] {'mp'}, use_global_device_ids=true, to_apply=%region_2.0 | all-reduce | flops 128 | bytes 1024 | tf_op jit(solution)/shard_map/psum | solution.py:43
  67.1 24.9 %all-gather.3.cloned.1.call-done = bf16[128,4096]{1,0:T(8,128)(2,1)} async-done(((bf16[128,512]{1,0:T(8,128)(2,1)}), bf16[128,4096]{1,0:T(8,128)(2,1)}) %all-gather.3.cloned.1.call-update) | async-done | bytes 1048592 | tf_op jit(solution)/shard_map/all_gather | solution.py:52
  91.9 3.2 fusion.9
  96.2 3.4 fusion.41
  100.3 32.6 %reduce-scatter.6.cloned.1.call-done = f32[128,512]{1,0:T(8,128)} async-done(((f32[128,4096]{1,0:T(8,128)}), f32[128,512]{1,0:T(8,128)}) %reduce-scatter.6.cloned.1.call-update) | async-done | bytes 262160 | tf_op jit(solution)/shard_map/reduce_scatter | solution.py:73
  133.9 15.0 %psum.22 = f32[128]{0:T(128)S(1)} all-reduce(f32[128]{0:T(128)S(1)} %multiply_reduce_fusion.1), channel_id=1, replica_groups=mesh['dp'=32,'mp'=8] {'mp'}, use_global_device_ids=true, to_apply=%region_10.11 | all-reduce | flops 128 | bytes 1024 | tf_op jit(solution)/shard_map/psum | solution.py:78
  148.9 1.7 fusion.24
  152.2 24.3 %all-gather.5.cloned.1.call-done = bf16[128,4096]{1,0:T(8,128)(2,1)} async-done(((bf16[128,512]{1,0:T(8,128)(2,1)}), bf16[128,4096]{1,0:T(8,128)(2,1)}) %all-gather.5.cloned.1.call-update) | async-done | bytes 1048592 | tf_op jit(solution)/shard_map/all_gather | solution.py:93
  176.4 4.7 broadcast_in_dim.19
  181.1 4.1 reshape.149
  185.2 3.4 broadcast_in_dim.18
  188.7 67.4 %scatter_fusion = bf16[32,24,4096]{2,1,0:T(8,128)(2,1)} fusion(bf16[32,24,4096]{2,1,0:T(8,128)(2,1)} %broadcast_in_dim.18, s32[256]{0:T(256)S(1)} %bitcast.69, bf16[256,4096]{1,0:T(8,128)(2,1)} %reshape.149), kind=kCustom, calls=%fused_computation.1 | custom fusion | bytes 6293504 | tf_op jit(solution)/shard_map/scatter | solution.py:97
  256.1 148.8 %all_to_all.10 = bf16[32,24,4096]{2,1,0:T(8,128)(2,1)S(1)} all-to-all(bf16[32,24,4096]{2,1,0:T(8,128)(2,1)} %scatter_fusion), channel_id=1, replica_groups=mesh['dp'=32,'mp'=8] {'dp'}, dimensions={0} | all-to-all | bytes 12582912 | tf_op jit(solution)/shard_map/all_to_all | solution.py:99
  404.9 1.9 fusion.20
  406.8 6.3 fusion.1
  413.1 6.3 all-to-all-start.1
  419.8 23.0 %psum.23 = f32[128,32]{0,1:T(8,128)S(1)} all-reduce(f32[128,32]{0,1:T(8,128)S(1)} %fusion.23), channel_id=1, replica_groups=mesh['dp'=32,'mp'=8] {'mp'}, use_global_device_ids=true, to_apply=%region_12.13 | all-reduce | flops 4096 | bytes 32768 | tf_op jit(solution)/shard_map/psum | solution.py:80
  443.0 255.6 %all-to-all-done.1 = f32[32,24,4096]{2,1,0:T(8,128)} async-done(((f32[32,24,4096]{2,1,0:T(8,128)}), f32[32,24,4096]{2,1,0:T(8,128)}, u32[]{:S(2)}, u32[]{:S(2)}) %all-to-all-start.1) | async-done | bytes 12582944 | tf_op jit(solution)/shard_map/all_to_all | solution.py:108
  698.6 7.6 gather_fusion
  706.2 5.8 reshape.140
  712.0 10.0 %multiply_reduce_fusion = f32[128,4096]{1,0:T(8,128)} fusion(f32[128,2,4096]{2,1,0:T(2,128)} %reshape.140, f32[128,2]{1,0:T(8,128)S(1)} %copy.40), kind=kLoop, calls=%fused_computation.3 | loop fusion | flops 1572864 | bytes 6292480 | tf_op jit(solution)/shard_map/reduce_sum | solution.py:110
  722.1 48.8 %reduce-scatter.8.cloned.1.call-done = f32[128,512]{1,0:T(8,128)} async-done(((f32[128,4096]{1,0:T(8,128)}), f32[128,512]{1,0:T(8,128)}) %reduce-scatter.8.cloned.1.call-update) | async-done | bytes 262160 | tf_op jit(solution)/shard_map/reduce_scatter | solution.py:111
  (65 shorter events, 10.1 us)
Async XLA Ops:
  7.2 399.7 %copy-start = (bf16[1,256,4096]{2,1,0:T(8,128)(2,1)S(1)}, bf16[1,256,4096]{2,1,0:T(8,128)(2,1)}, u32[]{:S(2)}) copy-start(bf16[1,256,4096]{2,1,0:T(8,128)(2,1)} %param.27) | copy-start | bytes 6291460
  7.2 41.3 %reduce-scatter.4.cloned.1.call-start = ((), (), s32[]{:S(2)}) async-start(), calls=%async_computation.5 | async-start | bytes 2359296 | tf_op jit(solution)/shard_map/reduce_scatter | solution.py:40
  10.8 0.7 copy-start.8
  10.8 37.7 %copy-start.4 = (bf16[128,512]{1,0:T(8,128)(2,1)S(1)}, bf16[128,512]{1,0:T(8,128)(2,1)}, u32[]{:S(2)}) copy-start(bf16[128,512]{1,0:T(8,128)(2,1)} %param.15) | copy-start | bytes 393220
  10.8 55.5 %copy-start.5 = (bf16[128,256]{1,0:T(8,128)(2,1)S(1)}, bf16[128,256]{1,0:T(8,128)(2,1)}, u32[]{:S(2)}) copy-start(bf16[128,256]{1,0:T(8,128)(2,1)} %param.19) | copy-start | bytes 196612
  10.8 81.1 %all-gather.3.cloned.1.call-start = ((), (), s32[]{:S(2)}) async-start(), calls=%async_computation.6 | async-start | bytes 1179648 | tf_op jit(solution)/shard_map/all_gather | solution.py:52
  66.2 66.6 %reduce-scatter.6.cloned.1.call-start = ((), (), s32[]{:S(2)}) async-start(), calls=%async_computation.7 | async-start | bytes 2359296 | tf_op jit(solution)/shard_map/reduce_scatter | solution.py:73
  99.6 0.7 copy-start.9
  99.6 33.3 %copy-start.3 = (bf16[128,512]{1,0:T(8,128)(2,1)S(1)}, bf16[128,512]{1,0:T(8,128)(2,1)}, u32[]{:S(2)}) copy-start(bf16[128,512]{1,0:T(8,128)(2,1)} %param.20) | copy-start | bytes 393220
  99.6 51.1 %copy-start.7 = (s32[128,2]{0,1:T(2,128)S(1)}, s32[128,2]{0,1:T(2,128)}, u32[]{:S(2)}) copy-start(s32[128,2]{0,1:T(2,128)} %param.24) | copy-start | bytes 3076
  99.6 76.8 %all-gather.5.cloned.1.call-start = ((), (), s32[]{:S(2)}) async-start(), calls=%async_computation.8 | async-start | bytes 1179648 | tf_op jit(solution)/shard_map/all_gather | solution.py:93
  256.1 148.8 %copy-start.10 = (bf16[1,4096,256]{2,1,0:T(8,128)(2,1)S(1)}, bf16[1,4096,256]{2,1,0:T(8,128)(2,1)}, u32[]{:S(2)}) copy-start(bf16[1,4096,256]{2,1,0:T(8,128)(2,1)} %param.26) | copy-start | bytes 6291460
  413.1 6.4 copy-start.2
  413.1 6.4 copy-start.6
  413.1 285.5 %all-to-all-start.1 = ((f32[32,24,4096]{2,1,0:T(8,128)}), f32[32,24,4096]{2,1,0:T(8,128)}, u32[]{:S(2)}, u32[]{:S(2)}) async-start(f32[32,24,4096]{2,1,0:T(8,128)} %fusion.1), calls=%async_computation.3 | async-start | bytes 25165824 | tf_op jit(solution)/shard_map/all_to_all | solution.py:108
  419.4 351.5 %reduce-scatter.8.cloned.1.call-start = ((), (), s32[]{:S(2)}) async-start(), calls=%async_computation.9 | async-start | bytes 2359296 | tf_op jit(solution)/shard_map/reduce_scatter | solution.py:111
  712.0 60.5 %copy-start.1 = (bf16[1,256,4096]{2,1,0:T(8,128)(2,1)S(1)}, bf16[1,256,4096]{2,1,0:T(8,128)(2,1)}, u32[]{:S(2)}) copy-start(bf16[1,256,4096]{2,1,0:T(8,128)(2,1)} %param.27) | copy-start | bytes 6291460
Sparse Core Ops, SparseCore 0:
  10.9 37.4 reduce-scatter.3
  66.3 25.5 all-gather.2
  99.7 33.0 reduce-scatter.5
  150.8 25.6 all-gather.4
  722.2 48.6 reduce-scatter.7
where the time goes:
time: 782 us; the launch traced here: 779 us
  waiting for transfers between devices  423 us (54%)
  blocking collectives  202 us (26%)
  local copies, waits for them, and re-layouts  95.5 us (12%)
  matrix products  19.4 us (2%)
  other arithmetic  18.1 us (2%)
  between operations  14.6 us (2%)
    all_to_all x1, waiting for transfers between devices, local(): lax.all_to_all(result, 'dp', split_axis=0, concat_axis=0, tiled=True)  256 us
    all_to_all x1, blocking collectives, local(): lax.all_to_all(packed, 'dp', split_axis=0, concat_axis=0, tiled=True)  149 us
    scatter x1, local copies, waits for them, and re-layouts, local(): packed = jnp.zeros((expert_count, capacity, full_width), jnp.bfloat16).at...  67.4 us
    reduce_scatter x1, waiting for transfers between devices, local(): moe = lax.psum_scatter(moe_part, 'mp', scatter_dimension=1, tiled=True)  48.8 us
    reduce_scatter x1, waiting for transfers between devices, local(): lax.psum_scatter(text_part, 'mp', scatter_dimension=1, tiled=True)  37 us
    reduce_scatter x1, waiting for transfers between devices, local(): lax.psum_scatter(cross_part, 'mp', scatter_dimension=1, tiled=True)  32.6 us
    all_gather x1, waiting for transfers between devices, local(): lax.all_gather(encoded, 'mp', axis=1, tiled=True)  24.9 us
    all_gather x1, waiting for transfers between devices, local(): full_rows = lax.all_gather(normed, 'mp', axis=1, tiled=True)  24.3 us
  transfers between devices with their start and end apart: 6, of which 6 were waited for; matrix products, arithmetic and copies ran while one was open for 0% of the time, Pallas kernels for 0%

commit v1 on v0

v1 whole, which is shorter than its diff:
```python
import functools
import jax
import jax.numpy as jnp
from jax import lax
from jax.experimental import pallas as pl
from jax.experimental.pallas import tpu as pltpu
from jax.sharding import PartitionSpec as P

HD = 64
EPSILON = 1e-06
SCORE_SCALE = 0.125
MESH = pl.DeviceIdType.MESH
NZ, NY, NX = 8, 4, 4
N_DP, N_MP = NZ * NY, NX * 2
EXPERTS = 32
WIDTH = 4096
SLICE = WIDTH // N_MP
ROWS = 128
FF_SLICE = 256
MSG_ROWS, MSG_LANES = 16, 768
HALF = SLICE // 2
CHUNKS = 8
PER = N_DP // CHUNKS
F32, BF16 = jnp.float32, jnp.bfloat16


def remote(src, dst, send, recv, device):
    return pltpu.make_async_remote_copy(
        src_ref=src, dst_ref=dst, send_sem=send, recv_sem=recv, device_id=device, device_id_type=MESH
    )


def offset_of(order):
    turn = order // NY
    odd = turn % 2
    dz = (1 - odd) * (turn // 2) + odd * (NZ - (turn + 1) // 2)
    return dz, order % NY


def moe_kernel(
    hidden, gain, stats, ids_col, ids_row, w_in_hbm, w_out_hbm,
    mixed,
    w_in, w_out, packed, full, give, kept, taken, half_l, half_r, sum_l, sum_r, done, back,
    load_sem, disp_send, disp_recv, ag_send, ag_recv, rs_send, rs_recv, ret_send, ret_recv,
):
    dp, mp = lax.axis_index("dp"), lax.axis_index("mp")
    z, y = dp // NY, dp % NY
    x, core = mp // 2, mp % 2
    x_right, x_left, x_far = (x + 1) % NX, (x + NX - 1) % NX, (x + 2) % NX
    sibling = (dp, x * 2 + 1 - core)
    right, left = (dp, x_right * 2 + core), (dp, x_left * 2 + core)
    m_right, m_left, m_far = x_right * 2 + core, x_left * 2 + core, x_far * 2 + core
    half = PER // 2

    def dest_of(order):
        dz, dy = offset_of(order)
        return ((z + dz) % NZ) * NY + (y + dy) % NY

    def origin_of(order):
        dz, dy = offset_of(order)
        return ((z + NZ - dz) % NZ) * NY + (y + NY - dy) % NY

    barrier = pltpu.get_barrier_semaphore()

    def greet(order, carry):
        pl.semaphore_signal(barrier, inc=1, device_id=(dest_of(order), mp), device_id_type=MESH)
        return carry

    lax.fori_loop(1, N_DP, greet, 0)
    for device in (sibling, right, left):
        pl.semaphore_signal(barrier, inc=1, device_id=device, device_id_type=MESH)
    load_in = pltpu.make_async_copy(w_in_hbm, w_in, load_sem.at[0])
    load_out = pltpu.make_async_copy(w_out_hbm, w_out, load_sem.at[1])
    load_in.start()
    load_out.start()

    table = jnp.transpose(jnp.concatenate([stats[...], jnp.zeros((ROWS - stats.shape[0], ROWS), F32)], axis=0))
    rms = lax.rsqrt(table[:, EXPERTS:EXPERTS + 1] / WIDTH + EPSILON)
    normed = (hidden[...] * gain[...].astype(F32) * rms).astype(BF16)

    row_at = lax.broadcasted_iota(jnp.int32, (ROWS, ROWS), 0)
    col_at = lax.broadcasted_iota(jnp.int32, (ROWS, ROWS), 1)
    expert_row = lax.broadcasted_iota(jnp.int32, (EXPERTS, ROWS), 0)
    named_row = [jnp.where(expert_row == ids_row[k:k + 1, :], 1.0, 0.0) for k in range(2)]
    earlier_row = jnp.dot(
        (named_row[0] + named_row[1]).astype(BF16),
        jnp.where(row_at < col_at, 1.0, 0.0).astype(BF16),
        preferred_element_type=F32,
    )
    message = lax.broadcasted_iota(jnp.int32, (EXPERTS * MSG_ROWS, ROWS), 0)
    upper = (message // 8) % 2
    pick_head = jnp.zeros((EXPERTS * MSG_ROWS, ROWS), F32)
    pick_tail = jnp.zeros((EXPERTS * MSG_ROWS, ROWS), F32)
    for k in range(2):
        slot = jnp.sum(named_row[k] * earlier_row, axis=0, keepdims=True).astype(jnp.int32)
        base = ids_row[k:k + 1, :] * MSG_ROWS
        head_at = jnp.where(slot < MSG_ROWS, base + slot, -1)
        tail_at = jnp.where(slot >= MSG_ROWS, base + slot - MSG_ROWS, -1)
        pick_head = pick_head + jnp.where(message == head_at, 1.0, 0.0)
        pick_tail = pick_tail + jnp.where(message - 8 * upper == tail_at, 1.0, 0.0)
    head = jnp.dot(pick_head.astype(BF16), normed, preferred_element_type=F32)
    packed[:, :, 0:SLICE] = head.astype(BF16).reshape(EXPERTS, MSG_ROWS, SLICE)
    tail = jnp.dot(pick_tail.astype(BF16), normed, preferred_element_type=F32)
    tail = jnp.where(upper[:, 0:1] == 0, tail[:, 0:HALF], tail[:, HALF:SLICE])
    packed[:, :, SLICE:MSG_LANES] = tail.astype(BF16).reshape(EXPERTS, MSG_ROWS, HALF)

    pl.semaphore_wait(barrier, N_DP - 1 + 3)

    own = pltpu.make_async_copy(packed.at[dp], full.at[mp, 0, 0], disp_recv.at[0])
    own.start()

    def dispatch(order, carry):
        dest = dest_of(order)
        chunk, place = order // PER, order % PER
        remote(packed.at[dest], full.at[mp, chunk, place], disp_send, disp_recv.at[chunk], (dest, mp)).start()
        return carry

    lax.fori_loop(1, N_DP, dispatch, 0)

    def gather_copy(kind, k):
        src = {
            0: (mp, None, sibling), 1: (mp, None, right), 2: (mp, None, left),
            3: (m_left, 0, right), 4: (m_right, half, left),
            5: (m_left, None, sibling), 6: (m_right, None, sibling), 7: (m_far, None, sibling),
        }[kind]
        place, part, device = src
        ref = full.at[place, k] if part is None else full.at[place, k, pl.ds(part, half)]
        return remote(ref, ref, ag_send.at[kind, k], ag_recv.at[kind, k], device)

    def sum_copy(kind, k):
        src, dst, device = {
            0: (give.at[k], taken.at[k], sibling),
            1: (kept.at[k, x_far, pl.ds(0, half)], half_l.at[k], right),
            2: (kept.at[k, x_far, pl.ds(half, half)], half_r.at[k], left),
            3: (kept.at[k, x_right], sum_l.at[k], right),
            4: (kept.at[k, x_left], sum_r.at[k], left),
        }[kind]
        return remote(src, dst, rs_send.at[kind, k], rs_recv.at[kind, k], device)

    def arrive(k):
        pltpu.make_async_copy(full.at[mp, k], full.at[mp, k], disp_recv.at[k]).wait()
        for kind in (1, 2, 0):
            gather_copy(kind, k).start()

    def forward(k):
        gather_copy(1, k).wait_recv()
        gather_copy(3, k).start()
        gather_copy(2, k).wait_recv()
        gather_copy(4, k).start()
        gather_copy(5, k).start()
        gather_copy(6, k).start()

    def forward_far(k):
        gather_copy(3, k).wait_recv()
        gather_copy(4, k).wait_recv()
        gather_copy(7, k).start()

    def compute(k):
        for kind in (0, 5, 6, 7):
            gather_copy(kind, k).wait_recv()

        @pl.when(k == 0)
        def _():
            load_in.wait()
            load_out.wait()

        rows = PER * MSG_ROWS
        low = jnp.zeros((2 * rows, FF_SLICE), F32)
        high = jnp.zeros((2 * rows, FF_SLICE), F32)
        for s in range(N_MP):
            block = full[s, k].reshape(rows, MSG_LANES)
            end = block[:, SLICE:]
            low = low + jnp.dot(
                jnp.concatenate([block[:, 0:HALF], end], axis=0),
                w_in[s * SLICE:s * SLICE + HALF, :],
                preferred_element_type=F32,
            )
            high = high + jnp.dot(
                jnp.concatenate([block[:, HALF:SLICE], end], axis=0),
                w_in[s * SLICE + HALF:(s + 1) * SLICE, :],
                preferred_element_type=F32,
            )
        ends = (
            low[rows:].reshape(PER, MSG_ROWS, FF_SLICE)[:, 0:8]
            + high[rows:].reshape(PER, MSG_ROWS, FF_SLICE)[:, 8:16]
        )
        before = jnp.concatenate([low[:rows] + high[:rows], ends.reshape(PER * 8, FF_SLICE)], axis=0)
        inner = jax.nn.gelu(before, approximate=True).astype(BF16)

        def result(ref, px, side):
            at = pl.multiple_of((px * 2 + side) * SLICE, SLICE)
            out = jnp.dot(inner, w_out[:, pl.ds(at, SLICE)], preferred_element_type=F32)
            ref[k, px, :, :, 0:SLICE] = out[:rows].astype(BF16).reshape(PER, MSG_ROWS, SLICE)
            ends = out[rows:].reshape(PER, 8, SLICE)
            ends = jnp.concatenate([ends[:, :, 0:HALF], ends[:, :, HALF:SLICE]], axis=1)
            ref[k, px, :, :, SLICE:MSG_LANES] = ends.astype(BF16)

        for px in range(NX):
            result(give, px, 1 - core)
        sum_copy(0, k).start()
        for px in range(NX):
            result(kept, px, core)

    def pair(k, px, part=slice(None)):
        return kept[k, px, part].astype(F32) + taken[k, px, part].astype(F32)

    def add_sibling(k):
        sum_copy(0, k).wait_recv()
        kept[k, x_far] = pair(k, x_far).astype(BF16)
        sum_copy(1, k).start()
        sum_copy(2, k).start()

    def add_far(k):
        first, second = slice(0, half), slice(half, PER)
        sum_copy(1, k).wait_recv()
        kept[k, x_right, first] = (pair(k, x_right, first) + half_l[k].astype(F32)).astype(BF16)
        kept[k, x_right, second] = pair(k, x_right, second).astype(BF16)
        sum_copy(3, k).start()
        sum_copy(2, k).wait_recv()
        kept[k, x_left, first] = pair(k, x_left, first).astype(BF16)
        kept[k, x_left, second] = (pair(k, x_left, second) + half_r[k].astype(F32)).astype(BF16)
        sum_copy(4, k).start()

    def finish(k):
        sum_copy(3, k).wait_recv()
        sum_copy(4, k).wait_recv()
        done[k] = (pair(k, x) + sum_l[k].astype(F32) + sum_r[k].astype(F32)).astype(BF16)
        for j in range(PER):
            order = k * PER + j
            origin = origin_of(order)
            if j == 0:
                @pl.when(k == 0)
                def _():
                    pltpu.make_async_copy(done.at[k, j], back.at[dp], ret_recv).start()

                @pl.when(k > 0)
                def _():
                    remote(done.at[k, j], back.at[dp], ret_send, ret_recv, (origin, mp)).start()
            else:
                remote(done.at[k, j], back.at[dp], ret_send, ret_recv, (origin, mp)).start()
        for kind in range(8):
            gather_copy(kind, k).wait_send()
        for kind in range(5):
            sum_copy(kind, k).wait_send()

    stages = (arrive, forward, forward_far, compute, add_sibling, add_far, finish)

    def step(i, carry):
        for lag, stage in enumerate(stages):
            @pl.when((i >= lag) & (i - lag < CHUNKS))
            def _():
                stage(i - lag)
        return carry

    lax.fori_loop(0, CHUNKS + len(stages) - 1, step, 0)

    expert_col = lax.broadcasted_iota(jnp.int32, (ROWS, EXPERTS), 1)
    named_col = [jnp.where(expert_col == ids_col[:, k:k + 1], 1.0, 0.0) for k in range(2)]
    earlier_col = jnp.dot(
        jnp.where(col_at < row_at, 1.0, 0.0).astype(BF16),
        (named_col[0] + named_col[1]).astype(BF16),
        preferred_element_type=F32,
    )
    logits = [rms * jnp.sum(named_col[k] * table[:, 0:EXPERTS], axis=1, keepdims=True) for k in range(2)]
    top = jnp.maximum(logits[0], logits[1])
    raised = [jnp.exp(value - top) for value in logits]
    place = lax.broadcasted_iota(jnp.int32, (ROWS, EXPERTS * MSG_ROWS), 1)
    gate_head = jnp.zeros(place.shape, F32)
    gate_low = jnp.zeros(place.shape, F32)
    gate_high = jnp.zeros(place.shape, F32)
    for k in range(2):
        gate = raised[k] / (raised[0] + raised[1])
        slot = jnp.sum(named_col[k] * earlier_col, axis=1, keepdims=True).astype(jnp.int32)
        base = ids_col[:, k:k + 1] * MSG_ROWS
        head_at = jnp.where(slot < MSG_ROWS, base + slot, -1)
        tail_at = jnp.where(slot >= MSG_ROWS, base + slot - MSG_ROWS, -100)
        gate_head = gate_head + jnp.where(place == head_at, gate, 0.0)
        gate_low = gate_low + jnp.where(place == tail_at, gate, 0.0)
        gate_high = gate_high + jnp.where(place == tail_at + 8, gate, 0.0)

    pltpu.make_async_copy(back, back, ret_recv).wait()

    def weigh(weights, values):
        main = weights.astype(BF16)
        rest = (weights - main.astype(F32)).astype(BF16)
        return jnp.dot(main, values, preferred_element_type=F32) + jnp.dot(
            rest, values, preferred_element_type=F32
        )

    results = back[...].reshape(EXPERTS * MSG_ROWS, MSG_LANES)
    ends = results[:, SLICE:]
    moe = weigh(gate_head, results[:, 0:SLICE])
    mixed[:, 0:HALF] = (hidden[:, 0:HALF] + moe[:, 0:HALF] + weigh(gate_low, ends)).astype(BF16)
    mixed[:, HALF:] = (hidden[:, HALF:] + moe[:, HALF:] + weigh(gate_high, ends)).astype(BF16)

    most = packed.at[pl.ds(0, N_DP - 1)]
    remote(most, most, disp_send, disp_recv.at[0], sibling).wait_send()
    remote(most, most, ret_send, ret_recv, sibling).wait_send()


def moe_call(hidden, gain, stats, ids, w_in, w_out):
    block = (PER, MSG_ROWS, MSG_LANES)
    vmem = pl.BlockSpec(memory_space=pltpu.VMEM)
    hbm = pl.BlockSpec(memory_space=pl.ANY)
    dma = pltpu.SemaphoreType.DMA
    return pl.pallas_call(
        moe_kernel,
        out_shape=jax.ShapeDtypeStruct((ROWS, SLICE), BF16),
        in_specs=[vmem] * 5 + [hbm] * 2,
        out_specs=vmem,
        scratch_shapes=[
            pltpu.VMEM((WIDTH, FF_SLICE), BF16),
            pltpu.VMEM((FF_SLICE, WIDTH), BF16),
            pltpu.VMEM((EXPERTS, MSG_ROWS, MSG_LANES), BF16),
            pltpu.VMEM((N_MP, CHUNKS) + block, BF16),
            pltpu.VMEM((CHUNKS, NX) + block, BF16),
            pltpu.VMEM((CHUNKS, NX) + block, BF16),
            pltpu.VMEM((CHUNKS, NX) + block, BF16),
            pltpu.VMEM((CHUNKS, PER // 2, MSG_ROWS, MSG_LANES), BF16),
            pltpu.VMEM((CHUNKS, PER // 2, MSG_ROWS, MSG_LANES), BF16),
            pltpu.VMEM((CHUNKS,) + block, BF16),
            pltpu.VMEM((CHUNKS,) + block, BF16),
            pltpu.VMEM((CHUNKS,) + block, BF16),
            pltpu.VMEM((EXPERTS, MSG_ROWS, MSG_LANES), BF16),
            dma((2,)),
            dma,
            dma((CHUNKS,)),
            dma((8, CHUNKS)),
            dma((8, CHUNKS)),
            dma((5, CHUNKS)),
            dma((5, CHUNKS)),
            dma,
            dma,
        ],
        compiler_params=pltpu.CompilerParams(
            collective_id=2, has_side_effects=True, vmem_limit_bytes=56 * 2**20
        ),
        name="experts",
    )(hidden, gain.reshape(1, SLICE), stats, ids, ids.T, w_in, w_out)


def local(
    enc_context, enc_resid, enc_out_w, final_gain, kv_weight, img_queries, img_resid, dec_out_w,
    moe_gain, router_w, expert_ids, text_lengths, expert_in, expert_out,
):
    full_width = enc_out_w.shape[1]
    text_part = jnp.dot(enc_context, enc_out_w, preferred_element_type=jnp.float32)
    text_state = enc_resid.astype(jnp.float32) + lax.psum_scatter(
        text_part, "mp", scatter_dimension=1, tiled=True
    )
    text_square = lax.psum(jnp.sum(text_state * text_state, axis=1), "mp")
    text_scale = lax.rsqrt(text_square / full_width + EPSILON)
    encoded = (text_state * final_gain.astype(jnp.float32) * text_scale[:, None]).astype(
        jnp.bfloat16
    )
    heads_width = kv_weight.shape[2]
    text_count = encoded.shape[0]
    kv_sums = jnp.einsum(
        "tf,cfh->cth",
        lax.all_gather(encoded, "mp", axis=1, tiled=True),
        kv_weight,
        preferred_element_type=jnp.float32,
    )
    key_rows = kv_sums[0].astype(jnp.bfloat16)
    value_rows = kv_sums[1].astype(jnp.bfloat16)
    row_count = img_queries.shape[0]
    head_count = heads_width // HD
    query_heads = img_queries.reshape(row_count, head_count, HD)
    key_heads = key_rows.reshape(text_count, head_count, HD)
    value_heads = value_rows.reshape(text_count, head_count, HD)
    scores = (
        jnp.einsum("qhd,khd->hqk", query_heads, key_heads, preferred_element_type=jnp.float32)
        * SCORE_SCALE
    )
    valid = jnp.arange(text_count, dtype=jnp.int32)[None, None, :] < text_lengths[0]
    scores = jnp.where(valid, scores, -jnp.inf)
    probs = jax.nn.softmax(scores, axis=-1).astype(jnp.bfloat16)
    context = jnp.einsum("hqk,khd->qhd", probs, value_heads, preferred_element_type=jnp.float32)
    context = context.reshape(row_count, heads_width).astype(jnp.bfloat16)
    cross_part = jnp.dot(context, dec_out_w, preferred_element_type=jnp.float32)
    hidden = img_resid.astype(jnp.float32) + lax.psum_scatter(
        cross_part, "mp", scatter_dimension=1, tiled=True
    )
    gained = hidden * moe_gain.astype(jnp.float32)
    square_part = jnp.sum(hidden * hidden, axis=1)
    logit_part = jnp.dot(gained, router_w.astype(jnp.float32), precision=lax.Precision.HIGHEST)
    part = jnp.concatenate(
        [logit_part.T, square_part[None, :], jnp.zeros((7, row_count), jnp.float32)], axis=0
    )
    stats = lax.psum(part, "mp")
    mixed = moe_call(hidden, moe_gain, stats, expert_ids, expert_in[0], expert_out[0])
    return (encoded, mixed)


def solution(mesh):
    placed = (
        P("dp", "mp"),
        P("dp", "mp"),
        P("mp", None),
        P("mp"),
        P(None, None, "mp"),
        P("dp", "mp"),
        P("dp", "mp"),
        P("mp", None),
        P("mp"),
        P("mp", None),
        P("dp", None),
        P("dp"),
        P("dp", None, "mp"),
        P("dp", "mp", None),
    )
    return jax.shard_map(
        local, mesh=mesh, in_specs=placed, out_specs=(P("dp", "mp"), P("dp", "mp")), check_vma=False
    )
```

time: 782 us -> 251 us (0.32)
  waiting for transfers between devices: 423 us -> 93 us
  blocking collectives: 202 us -> 39.3 us
  local copies, waits for them, and re-layouts: 95.5 us -> 6.14 us
  Pallas kernels: 0 us -> 80.1 us
  other arithmetic: 18.1 us -> 3.92 us
  matrix products: 19.4 us -> 10.3 us
    all_to_all x1 -> x0, waiting for transfers between devices: 256 us -> none  [local(): lax.all_to_all(result, 'dp', split_axis=0, concat_axis=0, tiled=True)]
    all_to_all x1 -> x0, blocking collectives: 149 us -> none  [local(): lax.all_to_all(packed, 'dp', split_axis=0, concat_axis=0, tiled=True)]
    pallas_call x0 -> x1, Pallas kernels: none -> 80.1 us  [moe_call(): pl.pallas_call(moe_kernel, out_shape=jax.ShapeDtypeStruct((ROWS, SLICE),...]
    scatter x1 -> x0, local copies, waits for them, and re-layouts: 67.4 us -> none  [local(): packed = jnp.zeros((expert_count, capacity, full_width), jnp.bfloat16).at...]
    reduce_scatter x1 -> x0, waiting for transfers between devices: 48.8 us -> none  [local(): moe = lax.psum_scatter(moe_part, 'mp', scatter_dimension=1, tiled=True)]
    all_gather x1 -> x0, waiting for transfers between devices: 24.3 us -> none  [local(): full_rows = lax.all_gather(normed, 'mp', axis=1, tiled=True)]
    psum x2 -> x1, blocking collectives: 38 us -> 24.4 us  [local(): stats = lax.psum(part, 'mp')]
    reduce_sum x5 -> x1, other arithmetic: 11.2 us -> 1.07 us  [local(): square_part = jnp.sum(hidden * hidden, axis=1)]
  transfers between devices with their start and end apart: 6 -> 3, of which waited for: 6 -> 3; matrix products, arithmetic and copies ran while one was open for 0% -> 1% of each run, Pallas kernels for 0% -> 0%
where the time goes in v1:
time: 251 us; the launch traced here: 247 us
  waiting for transfers between devices  93 us (37%)
  Pallas kernels  80.1 us (32%)
  blocking collectives  39.3 us (16%)
  between operations  14.5 us (6%)
  matrix products  10.3 us (4%)
  local copies, waits for them, and re-layouts  6.14 us (2%)
  other arithmetic  3.92 us (2%)
    pallas_call x1, Pallas kernels, moe_call(): pl.pallas_call(moe_kernel, out_shape=jax.ShapeDtypeStruct((ROWS, SLICE),...  80.1 us
    reduce_scatter x1, waiting for transfers between devices, local(): lax.psum_scatter(text_part, 'mp', scatter_dimension=1, tiled=True)  36.9 us
    reduce_scatter x1, waiting for transfers between devices, local(): lax.psum_scatter(cross_part, 'mp', scatter_dimension=1, tiled=True)  31.2 us
    all_gather x1, waiting for transfers between devices, local(): lax.all_gather(encoded, 'mp', axis=1, tiled=True)  24.9 us
    psum x1, blocking collectives, local(): stats = lax.psum(part, 'mp')  24.4 us
    psum x1, blocking collectives, local(): text_square = lax.psum(jnp.sum(text_state * text_state, axis=1), 'mp')  15 us
    unnamed x21, local copies, waits for them, and re-layouts  5.23 us
  transfers between devices with their start and end apart: 3, of which 3 were waited for; matrix products, arithmetic and copies ran while one was open for 1% of the time, Pallas kernels for 0%

profile of v1, /device:TPU:1, one launch (start us, length us, event | category | flops | bytes accessed | tf_op | source)
XLA Modules:
  0.0 247.4 jit_solution(10289236953898773975)
XLA Ops:
  7.2 1.5 copy-done
  8.8 2.6 %fusion.14 = f32[128,4096]{1,0:T(8,128)} fusion(bf16[128,256]{1,0:T(8,128)(2,1)} %param.14, bf16[256,4096]{1,0:T(8,128)(2,1)S(1)} %copy-done), kind=kOutput, calls=%fused_computation.27 | convolution fusion | flops 268435456 | bytes 4259840 | tf_op jit(solution)/shard_map/dot_general | solution.py:347
  11.5 0.6 copy-done.8
  12.1 36.9 %reduce-scatter.3.cloned.1.call-done = f32[128,512]{1,0:T(8,128)} async-done(((f32[128,4096]{1,0:T(8,128)}), f32[128,512]{1,0:T(8,128)}) %reduce-scatter.3.cloned.1.call-update) | async-done | bytes 262160 | tf_op jit(solution)/shard_map/reduce_scatter | solution.py:348
  49.0 1.1 multiply_reduce_fusion.1
  50.1 15.0 %psum.14 = f32[128]{0:T(128)S(1)} all-reduce(f32[128]{0:T(128)S(1)} %multiply_reduce_fusion.1), channel_id=1, replica_groups=mesh['dp'=32,'mp'=8] {'mp'}, use_global_device_ids=true, to_apply=%region_2.0 | all-reduce | flops 128 | bytes 1024 | tf_op jit(solution)/shard_map/psum | solution.py:351
  65.0 1.7 multiply_convert_fusion
  66.8 0.1 copy.23
  67.6 24.9 %all-gather.2.cloned.1.call-done = bf16[128,4096]{1,0:T(8,128)(2,1)} async-done(((bf16[128,512]{1,0:T(8,128)(2,1)}), bf16[128,4096]{1,0:T(8,128)(2,1)}) %all-gather.2.cloned.1.call-update) | async-done | bytes 1048592 | tf_op jit(solution)/shard_map/all_gather | solution.py:360
  92.5 3.2 %fusion.5 = bf16[2,128,256]{2,1,0:T(8,128)(2,1)S(1)} fusion(bf16[2,4096,256]{2,1,0:T(8,128)(2,1)} %param.18, bf16[128,4096]{1,0:T(8,128)(2,1)} %all-gather.2.cloned.1.call-done), kind=kOutput, calls=%fused_computation.7 | convolution fusion | flops 536936448 | bytes 5373952 | tf_op jit(solution)/shard_map/tf,cfh->cth/dot_general | solution.py:358
  95.9 0.2 fusion.3
  96.1 0.3 fusion.13
  96.4 0.1 copy.21
  96.6 0.2 convolution_convert_fusion.1
  96.8 3.4 %fusion.15 = f32[128,4096]{1,0:T(8,128)} fusion(bf16[128,256]{0,1:T(8,128)(2,1)S(1)} %bitcast.43, bf16[256,4096]{1,0:T(8,128)(2,1)} %param.21), kind=kOutput, calls=%fused_computation.28 | convolution fusion | flops 268435456 | bytes 4259840 | tf_op jit(solution)/shard_map/dot_general | solution.py:380
  100.2 0.6 copy-done.6
  100.9 0.6 reshape.29.gain
  101.5 0.7 copy.25.ids_col
  102.3 31.2 %reduce-scatter.5.cloned.1.call-done = f32[128,512]{1,0:T(8,128)} async-done(((f32[128,4096]{1,0:T(8,128)}), f32[128,512]{1,0:T(8,128)}) %reduce-scatter.5.cloned.1.call-update) | async-done | bytes 262160 | tf_op jit(solution)/shard_map/reduce_scatter | solution.py:381
  133.5 1.1 multiply_reduce_fusion
  134.6 0.3 convolution_bitcast_fusion
  134.9 24.4 %psum.15.stats = f32[40,128]{1,0:T(8,128)} all-reduce(f32[40,128]{1,0:T(8,128)S(1)} %maximum_maximum_fusion), channel_id=1, replica_groups=mesh['dp'=32,'mp'=8] {'mp'}, use_global_device_ids=true, to_apply=%region_7.8 | all-reduce | flops 5120 | bytes 40960 | tf_op jit(solution)/shard_map/psum | solution.py:390
  159.3 80.1 %experts.1 = bf16[128,512]{1,0:T(8,128)(2,1)} custom-call(f32[128,512]{1,0:T(8,128)} %copy-done.1, bf16[1,512]{1,0:T(2,128)(2,1)} %reshape.29.gain, f32[40,128]{1,0:T(8,128)} %psum.15.stats, s32[128,2]{1,0:T(8,128)} %copy.25.ids_col, s32[2,128]{1,0:T(2,128)} %bitcast.45, bf16[4096,256]{1,0:T(8,128)(2,1)} %bitcast.37, bf16[256,4096]{1,0:T(8,128)(2,1)} %bitcast.38), custom_call_target="tpu_custom_call" | custom-call | tf_op jit(solution)/shard_map/experts/pallas_call | solution.py:306
  239.3 1.6 copy.29
  (30 shorter events, 0.5 us)
Async XLA Ops:
  7.2 1.6 copy-start
  7.2 41.8 %reduce-scatter.3.cloned.1.call-start = ((), (), s32[]{:S(2)}) async-start(), calls=%async_computation.2 | async-start | bytes 2359296 | tf_op jit(solution)/shard_map/reduce_scatter | solution.py:348
  11.4 0.7 copy-start.8
  11.4 37.6 %copy-start.2 = (bf16[128,512]{1,0:T(8,128)(2,1)S(1)}, bf16[128,512]{1,0:T(8,128)(2,1)}, u32[]{:S(2)}) copy-start(bf16[128,512]{1,0:T(8,128)(2,1)} %param.15) | copy-start | bytes 393220
  11.4 55.4 %copy-start.4 = (bf16[128,256]{1,0:T(8,128)(2,1)S(1)}, bf16[128,256]{1,0:T(8,128)(2,1)}, u32[]{:S(2)}) copy-start(bf16[128,256]{1,0:T(8,128)(2,1)} %param.19) | copy-start | bytes 196612
  11.4 81.1 %all-gather.2.cloned.1.call-start = ((), (), s32[]{:S(2)}) async-start(), calls=%async_computation.3 | async-start | bytes 1179648 | tf_op jit(solution)/shard_map/all_gather | solution.py:360
  66.8 66.7 %reduce-scatter.5.cloned.1.call-start = ((), (), s32[]{:S(2)}) async-start(), calls=%async_computation.4 | async-start | bytes 2359296 | tf_op jit(solution)/shard_map/reduce_scatter | solution.py:381
  100.2 0.7 copy-start.6
  100.2 1.3 copy-start.7
  100.2 33.3 %copy-start.3 = (bf16[128,512]{1,0:T(8,128)(2,1)S(1)}, bf16[128,512]{1,0:T(8,128)(2,1)}, u32[]{:S(2)}) copy-start(bf16[128,512]{1,0:T(8,128)(2,1)} %param.20) | copy-start | bytes 393220
  100.2 34.3 %copy-start.5 = (bf16[512,32]{0,1:T(8,128)(2,1)S(1)}, bf16[512,32]{0,1:T(8,128)(2,1)}, u32[]{:S(2)}) copy-start(bf16[512,32]{0,1:T(8,128)(2,1)} %param.23) | copy-start | bytes 98308
  134.5 24.7 %copy-start.1 = (f32[128,512]{1,0:T(8,128)}, f32[128,512]{1,0:T(8,128)S(1)}, u32[]{:S(2)}) copy-start(f32[128,512]{1,0:T(8,128)S(1)} %get-tuple-element.3.hidden) | copy-start | bytes 786436
Sparse Core Ops, SparseCore 0:
  11.6 37.3 reduce-scatter.2
  66.9 25.5 all-gather.1
  100.3 33.0 reduce-scatter.4

commit v2 on v1

v2 whole, which is shorter than its diff:
```python
import functools
import jax
import jax.numpy as jnp
from jax import lax
from jax.experimental import pallas as pl
from jax.experimental.pallas import tpu as pltpu
from jax.sharding import PartitionSpec as P

HD = 64
EPSILON = 1e-06
SCORE_SCALE = 0.125
MESH = pl.DeviceIdType.MESH
NZ, NY, NX = 8, 4, 4
N_DP, N_MP = NZ * NY, NX * 2
EXPERTS = 32
WIDTH = 4096
SLICE = WIDTH // N_MP
ROWS = 128
FF_SLICE = 256
MSG_ROWS, MSG_LANES = 16, 768
HALF = SLICE // 2
CHUNKS = 8
PER = N_DP // CHUNKS
F32, BF16 = jnp.float32, jnp.bfloat16
VMEM_LIMIT = 56 * 2**20


def remote(src, dst, send, recv, device):
    return pltpu.make_async_remote_copy(
        src_ref=src, dst_ref=dst, send_sem=send, recv_sem=recv, device_id=device, device_id_type=MESH
    )


def offset_of(order):
    turn, place = order // PER, order % PER
    kind, odd = turn % 2, place % 2
    reach = 1 + kind + 2 * (place // 2)
    dz = ((1 - odd) * reach + odd * (NZ - reach)) * (1 - kind * (place // 3))
    return dz, turn // 2


PARTS = 2
PART = ROWS // PARTS
STATS = 40
AHEAD = 3
SELF = 7
LAGS = (0, 1, 2, 3, 4, 5, 6)


def kernel(*refs):
    sources, rest = refs[:14], refs[14:]
    (
        encoded, mixed,
        enc_context, enc_w, enc_resid, final_gain, kv_w, router, ids_row, img_queries, img_resid, moe_gain,
        lengths, dec_w, w_in, w_out,
        state, gathered, squares, tables, hidden, router_wide, picks, gated,
        enc_give, enc_kept, enc_taken, enc_half_l, enc_half_r, enc_sum_l, enc_sum_r,
        dec_give, dec_kept, dec_taken, dec_half_l, dec_half_r, dec_sum_l, dec_sum_r,
        packed, full, give, kept, taken, half_l, half_r, sum_l, sum_r, done, back,
        load_sem, enc_send, enc_recv, dec_send, dec_recv, ag_send, ag_recv,
        square_send, square_recv, table_send, table_recv,
        disp_send, disp_recv, slot_send, slot_recv, rs_send, rs_recv, ret_send, ret_recv,
    ) = rest
    targets = rest[2:16]
    dp, mp = lax.axis_index("dp"), lax.axis_index("mp")
    z, y = dp // NY, dp % NY
    x, core = mp // 2, mp % 2
    x_right, x_left, x_far = (x + 1) % NX, (x + NX - 1) % NX, (x + 2) % NX
    m_right, m_left, m_far = x_right * 2 + core, x_left * 2 + core, x_far * 2 + core
    sibling, right, left = (dp, x * 2 + 1 - core), (dp, m_right), (dp, m_left)

    def dest_of(order):
        dz, dy = offset_of(order)
        return ((z + dz) % NZ) * NY + (y + dy) % NY

    def origin_of(order):
        dz, dy = offset_of(order)
        return ((z + NZ - dz) % NZ) * NY + (y + NY - dy) % NY

    loads = [
        pltpu.make_async_copy(src, dst, load_sem.at[i])
        for i, (src, dst) in enumerate(zip(sources, targets))
    ]
    for load in loads[:3]:
        load.start()
    barrier = pltpu.get_barrier_semaphore()
    for o in range(1, N_MP):
        pl.semaphore_signal(barrier, inc=1, device_id=(dp, (mp + o) % N_MP), device_id_type=MESH)

    def greet(order, carry):
        pl.semaphore_signal(barrier, inc=1, device_id=(dest_of(order), mp), device_id_type=MESH)
        return carry

    lax.fori_loop(0, SELF, greet, 0)
    lax.fori_loop(SELF + 1, N_DP, greet, 0)
    for load in loads[3:]:
        load.start()

    def reduce_scatter(values, weights, resid, out, give, kept, taken, half_l, half_r, sum_l, sum_r, send, recv):
        half = PART // 2

        def copy(kind, r):
            src, dst, device = {
                0: (give.at[r], taken.at[r], sibling),
                1: (kept.at[r, x_far, pl.ds(0, half)], half_l.at[r], right),
                2: (kept.at[r, x_far, pl.ds(half, half)], half_r.at[r], left),
                3: (kept.at[r, x_right], sum_l.at[r], right),
                4: (kept.at[r, x_left], sum_r.at[r], left),
            }[kind]
            return remote(src, dst, send.at[kind, r], recv.at[kind, r], device)

        def product(ref, r, px, side):
            at = pl.multiple_of((px * 2 + side) * SLICE, SLICE)
            ref[r, px] = jnp.dot(
                values[r * PART:(r + 1) * PART], weights[:, pl.ds(at, SLICE)], preferred_element_type=F32
            ).astype(BF16)

        def pair(r, px, rows=slice(None)):
            return kept[r, px, rows].astype(F32) + taken[r, px, rows].astype(F32)

        for r in range(PARTS):
            for px in range(NX):
                product(give, r, px, 1 - core)
            if r == 0 and out is state:
                pl.semaphore_wait(barrier, N_MP - 1 + N_DP - 1)
            copy(0, r).start()
        for r in range(PARTS):
            for px in range(NX):
                product(kept, r, px, core)
        for r in range(PARTS):
            copy(0, r).wait_recv()
            kept[r, x_far] = pair(r, x_far).astype(BF16)
            copy(1, r).start()
            copy(2, r).start()
        first, second = slice(0, half), slice(half, PART)
        for r in range(PARTS):
            copy(1, r).wait_recv()
            kept[r, x_right, first] = (pair(r, x_right, first) + half_l[r].astype(F32)).astype(BF16)
            kept[r, x_right, second] = pair(r, x_right, second).astype(BF16)
            copy(3, r).start()
            copy(2, r).wait_recv()
            kept[r, x_left, first] = pair(r, x_left, first).astype(BF16)
            kept[r, x_left, second] = (pair(r, x_left, second) + half_r[r].astype(F32)).astype(BF16)
            copy(4, r).start()
        for r in range(PARTS):
            rows = slice(r * PART, (r + 1) * PART)
            base = resid[rows].astype(F32) + pair(r, x)
            copy(3, r).wait_recv()
            copy(4, r).wait_recv()
            out[rows] = base + sum_l[r].astype(F32) + sum_r[r].astype(F32)
            yield r

        def drain():
            for r in range(PARTS):
                for kind in range(5):
                    copy(kind, r).wait_send()

        drains.append(drain)

    drains = []

    def exchange(ref, send, recv):
        def copy(o):
            return remote(ref.at[mp], ref.at[mp], send.at[o], recv.at[mp], (dp, (mp + o) % N_MP))

        for o in range(1, N_MP):
            copy(o).start()

        def finish():
            for o in range(1, N_MP):
                other = ref.at[(mp + o) % N_MP]
                remote(other, other, send.at[o], recv.at[(mp + o) % N_MP], sibling).wait_recv()
            drains.append(lambda: [copy(o).wait_send() for o in range(1, N_MP)])

        return finish

    def gather_copy(kind):
        ref, device = {
            0: (gathered.at[mp, 0], sibling), 1: (gathered.at[mp, 1], sibling),
            2: (gathered.at[mp, 0], right), 3: (gathered.at[mp, 1], right),
            4: (gathered.at[mp, 0], left), 5: (gathered.at[mp, 1], left),
            6: (gathered.at[m_left, 0], right), 7: (gathered.at[m_right, 1], left),
            8: (gathered.at[m_left], sibling), 9: (gathered.at[m_right], sibling),
            10: (gathered.at[m_far], sibling),
        }[kind]
        return remote(ref, ref, ag_send.at[kind], ag_recv.at[kind], device)

    for load in loads[:4]:
        load.wait()
    text_gain = final_gain[...].astype(F32).reshape(1, SLICE)
    for r in reduce_scatter(
        enc_context[...], enc_w, enc_resid, state, enc_give, enc_kept, enc_taken, enc_half_l, enc_half_r,
        enc_sum_l, enc_sum_r, enc_send, enc_recv,
    ):
        gathered[mp, r] = (state[r * PART:(r + 1) * PART] * text_gain).astype(BF16)
        for kind in ((2, 4, 0), (5, 3, 1))[r]:
            gather_copy(kind).start()
    text_state = state[...]
    square = jnp.sum(text_state * text_state, axis=1, keepdims=True)
    squares[mp] = jnp.transpose(jnp.broadcast_to(square, (ROWS, ROWS)))[0:8]
    squares_done = exchange(squares, square_send, square_recv)

    for load in loads[4:]:
        load.wait()
    row_at = lax.broadcasted_iota(jnp.int32, (ROWS, ROWS), 0)
    col_at = lax.broadcasted_iota(jnp.int32, (ROWS, ROWS), 1)
    expert_row = lax.broadcasted_iota(jnp.int32, (EXPERTS, ROWS), 0)
    named_row = [jnp.where(expert_row == ids_row[k:k + 1, :], 1.0, 0.0) for k in range(2)]
    earlier_row = jnp.dot(
        (named_row[0] + named_row[1]).astype(BF16),
        jnp.where(row_at < col_at, 1.0, 0.0).astype(BF16),
        preferred_element_type=F32,
    )
    message = lax.broadcasted_iota(jnp.int32, (EXPERTS * MSG_ROWS, ROWS), 0)
    upper = (message // 8) % 2
    pick_head = jnp.zeros((EXPERTS * MSG_ROWS, ROWS), F32)
    pick_tail = jnp.zeros((EXPERTS * MSG_ROWS, ROWS), F32)
    slots = []
    for k in range(2):
        slot = jnp.sum(named_row[k] * earlier_row, axis=0, keepdims=True).astype(jnp.int32)
        slots.append(slot.astype(F32))
        base = ids_row[k:k + 1, :] * MSG_ROWS
        head_at = jnp.where(slot < MSG_ROWS, base + slot, -1)
        tail_at = jnp.where(slot >= MSG_ROWS, base + slot - MSG_ROWS, -1)
        pick_head = pick_head + jnp.where(message == head_at, 1.0, 0.0)
        pick_tail = pick_tail + jnp.where(message - 8 * upper == tail_at, 1.0, 0.0)
    picks[0] = pick_head.astype(BF16)
    picks[1] = pick_tail.astype(BF16)
    columns = jnp.transpose(
        jnp.concatenate([ids_row[...].astype(F32)] + slots + [jnp.zeros((ROWS - 4, ROWS), F32)], axis=0)
    )
    id_cols = [columns[:, k:k + 1].astype(jnp.int32) for k in range(2)]
    slot_cols = [columns[:, 2 + k:3 + k].astype(jnp.int32) for k in range(2)]
    router_wide[...] = jnp.zeros(router_wide.shape, F32)
    router_wide[0:EXPERTS] = router[...].astype(F32)

    sums = [jnp.zeros((ROWS, FF_SLICE), F32) for _ in range(2)]

    def project(m):
        at = pl.multiple_of(m * SLICE, SLICE)
        block = gathered[m].reshape(ROWS, SLICE)
        for which in range(2):
            sums[which] = sums[which] + jnp.dot(
                block, kv_w[which, pl.ds(at, SLICE), :], preferred_element_type=F32
            )

    project(mp)
    gather_copy(2).wait_recv()
    gather_copy(6).start()
    gather_copy(5).wait_recv()
    gather_copy(7).start()
    gather_copy(3).wait_recv()
    gather_copy(8).start()
    gather_copy(4).wait_recv()
    gather_copy(9).start()
    project(m_left)
    project(m_right)
    gather_copy(0).wait_recv()
    gather_copy(1).wait_recv()
    project(x * 2 + 1 - core)
    gather_copy(6).wait_recv()
    gather_copy(7).wait_recv()
    gather_copy(10).start()
    project(m_far)
    for kind, px in ((8, x_left), (9, x_right), (10, x_far)):
        gather_copy(kind).wait_recv()
        project(px * 2 + 1 - core)
    squares_done()
    total = squares[0]
    for m in range(1, N_MP):
        total = total + squares[m]
    total = jnp.transpose(jnp.concatenate([total, jnp.zeros((ROWS - 8, ROWS), F32)], axis=0))[:, 0:1]
    text_scale = lax.rsqrt(total / WIDTH + EPSILON)
    encoded[...] = (state[...] * text_gain * text_scale).astype(BF16)
    keys = (sums[0] * text_scale).astype(BF16)
    values = (sums[1] * text_scale).astype(BF16)

    heads = FF_SLICE // HD
    head_of = lax.broadcasted_iota(jnp.int32, (ROWS, FF_SLICE), 1) // HD
    queries = img_queries[...]
    alone = jnp.concatenate([jnp.where(head_of == h, queries, jnp.zeros_like(queries)) for h in range(heads)], axis=0)
    scores = SCORE_SCALE * lax.dot_general(
        alone, keys, (((1,), (1,)), ((), ())), preferred_element_type=F32
    )
    valid = lax.broadcasted_iota(jnp.int32, scores.shape, 1) < lengths[0]
    scores = jnp.where(valid, scores, -jnp.inf)
    raised = jnp.exp(scores - jnp.max(scores, axis=1, keepdims=True))
    probs = (raised / jnp.sum(raised, axis=1, keepdims=True)).astype(BF16)
    mixed_heads = jnp.dot(probs, values, preferred_element_type=F32)
    context = jnp.zeros((ROWS, FF_SLICE), F32)
    for h in range(heads):
        context = context + jnp.where(head_of == h, mixed_heads[h * ROWS:(h + 1) * ROWS], 0.0)
    context = context.astype(BF16)

    for _ in reduce_scatter(
        context, dec_w, img_resid, hidden, dec_give, dec_kept, dec_taken, dec_half_l, dec_half_r,
        dec_sum_l, dec_sum_r, dec_send, dec_recv,
    ):
        pass
    here = hidden[...]
    gained = here * moe_gain[...].astype(F32).reshape(1, SLICE)
    square = jnp.sum(here * here, axis=1, keepdims=True)
    logits = lax.dot_general(
        gained, router_wide[...], (((1,), (1,)), ((), ())),
        precision=lax.Precision.HIGHEST, preferred_element_type=F32,
    )
    lane = lax.broadcasted_iota(jnp.int32, (ROWS, ROWS), 1)
    tables[mp] = jnp.transpose(jnp.where(lane == EXPERTS, square, logits))[0:STATS]
    exchange(tables, table_send, table_recv)()
    total = tables[0]
    for m in range(1, N_MP):
        total = total + tables[m]
    table = jnp.transpose(jnp.concatenate([total, jnp.zeros((ROWS - STATS, ROWS), F32)], axis=0))
    rms = lax.rsqrt(table[:, EXPERTS:EXPERTS + 1] / WIDTH + EPSILON)
    normed = (gained * rms).astype(BF16)
    head = jnp.dot(picks[0], normed, preferred_element_type=F32)
    packed[:, :, 0:SLICE] = head.astype(BF16).reshape(EXPERTS, MSG_ROWS, SLICE)
    tail = jnp.dot(picks[1], normed, preferred_element_type=F32)
    upper = (lax.broadcasted_iota(jnp.int32, (EXPERTS * MSG_ROWS, ROWS), 0) // 8) % 2
    tail = jnp.where(upper[:, 0:1] == 0, tail[:, 0:HALF], tail[:, HALF:SLICE])
    packed[:, :, SLICE:MSG_LANES] = tail.astype(BF16).reshape(EXPERTS, MSG_ROWS, HALF)


    own = pltpu.make_async_copy(packed.at[dp], full.at[mp, SELF // PER, SELF % PER], disp_recv.at[SELF // PER])
    own.start()

    def dispatch(order, carry):
        dest = dest_of(order)
        chunk, place = order // PER, order % PER
        remote(packed.at[dest], full.at[mp, chunk, place], disp_send, disp_recv.at[chunk], (dest, mp)).start()
        return carry

    lax.fori_loop(0, SELF, dispatch, 0)
    lax.fori_loop(SELF + 1, AHEAD * PER, dispatch, 0)

    expert_col = lax.broadcasted_iota(jnp.int32, (ROWS, EXPERTS), 1)
    named_col = [jnp.where(expert_col == id_cols[k], 1.0, 0.0) for k in range(2)]
    logits = [rms * jnp.sum(named_col[k] * table[:, 0:EXPERTS], axis=1, keepdims=True) for k in range(2)]
    top = jnp.maximum(logits[0], logits[1])
    raised = [jnp.exp(value - top) for value in logits]
    place = lax.broadcasted_iota(jnp.int32, (ROWS, EXPERTS * MSG_ROWS), 1)
    gate_head = jnp.zeros(place.shape, F32)
    gate_low = jnp.zeros(place.shape, F32)
    gate_high = jnp.zeros(place.shape, F32)
    for k in range(2):
        gate = raised[k] / (raised[0] + raised[1])
        slot = slot_cols[k]
        base = id_cols[k] * MSG_ROWS
        head_at = jnp.where(slot < MSG_ROWS, base + slot, -1)
        tail_at = jnp.where(slot >= MSG_ROWS, base + slot - MSG_ROWS, -100)
        gate_head = gate_head + jnp.where(place == head_at, gate, 0.0)
        gate_low = gate_low + jnp.where(place == tail_at, gate, 0.0)
        gate_high = gate_high + jnp.where(place == tail_at + 8, gate, 0.0)

    for i, weights in enumerate((gate_head, gate_low, gate_high)):
        main = weights.astype(BF16)
        gated[2 * i] = main
        gated[2 * i + 1] = (weights - main.astype(F32)).astype(BF16)

    half = PER // 2

    def slot_copy(kind, k):
        src = {
            0: (mp, None, sibling), 1: (mp, None, right), 2: (mp, None, left),
            3: (m_left, 0, right), 4: (m_right, half, left),
            5: (m_left, None, sibling), 6: (m_right, None, sibling), 7: (m_far, None, sibling),
        }[kind]
        place, part, device = src
        ref = full.at[place, k] if part is None else full.at[place, k, pl.ds(part, half)]
        return remote(ref, ref, slot_send.at[kind, k], slot_recv.at[kind, k], device)

    def sum_copy(kind, k):
        src, dst, device = {
            0: (give.at[k], taken.at[k], sibling),
            1: (kept.at[k, x_far, pl.ds(0, half)], half_l.at[k], right),
            2: (kept.at[k, x_far, pl.ds(half, half)], half_r.at[k], left),
            3: (kept.at[k, x_right], sum_l.at[k], right),
            4: (kept.at[k, x_left], sum_r.at[k], left),
        }[kind]
        return remote(src, dst, rs_send.at[kind, k], rs_recv.at[kind, k], device)

    def arrive(k):
        @pl.when(k + AHEAD < CHUNKS)
        def _():
            first = (k + AHEAD) * PER
            lax.fori_loop(first, first + PER, dispatch, 0)

        pltpu.make_async_copy(full.at[mp, k], full.at[mp, k], disp_recv.at[k]).wait()
        for kind in (1, 2, 0):
            slot_copy(kind, k).start()

    def forward(k):
        slot_copy(1, k).wait_recv()
        slot_copy(3, k).start()
        slot_copy(2, k).wait_recv()
        slot_copy(4, k).start()
        slot_copy(5, k).start()
        slot_copy(6, k).start()

    def forward_far(k):
        slot_copy(3, k).wait_recv()
        slot_copy(4, k).wait_recv()
        slot_copy(7, k).start()

    def compute(k):
        for kind in (0, 5, 6, 7):
            slot_copy(kind, k).wait_recv()

        rows = PER * MSG_ROWS
        low = jnp.zeros((2 * rows, FF_SLICE), F32)
        high = jnp.zeros((2 * rows, FF_SLICE), F32)
        for s in range(N_MP):
            block = full[s, k].reshape(rows, MSG_LANES)
            end = block[:, SLICE:]
            low = low + jnp.dot(
                jnp.concatenate([block[:, 0:HALF], end], axis=0),
                w_in[s * SLICE:s * SLICE + HALF, :],
                preferred_element_type=F32,
            )
            high = high + jnp.dot(
                jnp.concatenate([block[:, HALF:SLICE], end], axis=0),
                w_in[s * SLICE + HALF:(s + 1) * SLICE, :],
                preferred_element_type=F32,
            )
        ends = (
            low[rows:].reshape(PER, MSG_ROWS, FF_SLICE)[:, 0:8]
            + high[rows:].reshape(PER, MSG_ROWS, FF_SLICE)[:, 8:16]
        )
        before = jnp.concatenate([low[:rows] + high[:rows], ends.reshape(PER * 8, FF_SLICE)], axis=0)
        inner = jax.nn.gelu(before, approximate=True).astype(BF16)

        def result(ref, px, side):
            at = pl.multiple_of((px * 2 + side) * SLICE, SLICE)
            out = jnp.dot(inner, w_out[:, pl.ds(at, SLICE)], preferred_element_type=F32)
            ref[k, px, :, :, 0:SLICE] = out[:rows].astype(BF16).reshape(PER, MSG_ROWS, SLICE)
            ends = out[rows:].reshape(PER, 8, SLICE)
            ends = jnp.concatenate([ends[:, :, 0:HALF], ends[:, :, HALF:SLICE]], axis=1)
            ref[k, px, :, :, SLICE:MSG_LANES] = ends.astype(BF16)

        for px in range(NX):
            result(give, px, 1 - core)
        sum_copy(0, k).start()
        for px in range(NX):
            result(kept, px, core)

    def pair(k, px, part=slice(None)):
        return kept[k, px, part].astype(F32) + taken[k, px, part].astype(F32)

    def add_sibling(k):
        sum_copy(0, k).wait_recv()
        kept[k, x_far] = pair(k, x_far).astype(BF16)
        sum_copy(1, k).start()
        sum_copy(2, k).start()

    def add_far(k):
        first, second = slice(0, half), slice(half, PER)
        sum_copy(1, k).wait_recv()
        kept[k, x_right, first] = (pair(k, x_right, first) + half_l[k].astype(F32)).astype(BF16)
        kept[k, x_right, second] = pair(k, x_right, second).astype(BF16)
        sum_copy(3, k).start()
        sum_copy(2, k).wait_recv()
        kept[k, x_left, first] = pair(k, x_left, first).astype(BF16)
        kept[k, x_left, second] = (pair(k, x_left, second) + half_r[k].astype(F32)).astype(BF16)
        sum_copy(4, k).start()

    def finish(k):
        sum_copy(3, k).wait_recv()
        sum_copy(4, k).wait_recv()
        done[k] = (pair(k, x) + sum_l[k].astype(F32) + sum_r[k].astype(F32)).astype(BF16)
        for j in range(PER):
            order = k * PER + j
            origin = origin_of(order)
            if j == SELF % PER:
                @pl.when(order == SELF)
                def _():
                    pltpu.make_async_copy(done.at[k, j], back.at[dp], ret_recv).start()

                @pl.when(order != SELF)
                def _():
                    remote(done.at[k, j], back.at[dp], ret_send, ret_recv, (origin, mp)).start()
            else:
                remote(done.at[k, j], back.at[dp], ret_send, ret_recv, (origin, mp)).start()
        for kind in range(8):
            slot_copy(kind, k).wait_send()
        for kind in range(5):
            sum_copy(kind, k).wait_send()

    stages = (arrive, forward, forward_far, compute, add_sibling, add_far, finish)

    def step(i, carry):
        for lag, stage in zip(LAGS, stages):
            @pl.when((i >= lag) & (i - lag < CHUNKS))
            def _():
                stage(i - lag)
        return carry

    lax.fori_loop(0, CHUNKS + LAGS[-1], step, 0)

    pltpu.make_async_copy(back, back, ret_recv).wait()

    def weigh(i, values):
        return jnp.dot(gated[2 * i], values, preferred_element_type=F32) + jnp.dot(
            gated[2 * i + 1], values, preferred_element_type=F32
        )

    results = back[...].reshape(EXPERTS * MSG_ROWS, MSG_LANES)
    ends = results[:, SLICE:]
    moe = weigh(0, results[:, 0:SLICE])
    mixed[:, 0:HALF] = (hidden[:, 0:HALF] + moe[:, 0:HALF] + weigh(1, ends)).astype(BF16)
    mixed[:, HALF:] = (hidden[:, HALF:] + moe[:, HALF:] + weigh(2, ends)).astype(BF16)

    most = packed.at[pl.ds(0, N_DP - 1)]
    remote(most, most, disp_send, disp_recv.at[0], sibling).wait_send()
    remote(most, most, ret_send, ret_recv, sibling).wait_send()


    for drain in drains:
        drain()
    for kind in range(11):
        gather_copy(kind).wait_send()


def call(*operands):
    vmem = pl.BlockSpec(memory_space=pltpu.VMEM)
    hbm = pl.BlockSpec(memory_space=pltpu.HBM)
    dma = pltpu.SemaphoreType.DMA
    block = (PER, MSG_ROWS, MSG_LANES)
    sums = [
        pltpu.VMEM((PARTS, NX, PART, SLICE), BF16),
        pltpu.VMEM((PARTS, NX, PART, SLICE), BF16),
        pltpu.VMEM((PARTS, NX, PART, SLICE), BF16),
        pltpu.VMEM((PARTS, PART // 2, SLICE), BF16),
        pltpu.VMEM((PARTS, PART // 2, SLICE), BF16),
        pltpu.VMEM((PARTS, PART, SLICE), BF16),
        pltpu.VMEM((PARTS, PART, SLICE), BF16),
    ]
    landing = [
        pltpu.SMEM(o.shape, o.dtype) if o.shape == (1,) else pltpu.VMEM(o.shape, o.dtype) for o in operands
    ]
    return pl.pallas_call(
        kernel,
        out_shape=(jax.ShapeDtypeStruct((ROWS, SLICE), BF16), jax.ShapeDtypeStruct((ROWS, SLICE), BF16)),
        in_specs=[hbm] * len(operands),
        out_specs=(vmem, vmem),
        scratch_shapes=landing + [
            pltpu.VMEM((ROWS, SLICE), F32),
            pltpu.VMEM((N_MP, PARTS, PART, SLICE), BF16),
            pltpu.VMEM((N_MP, 8, ROWS), F32),
            pltpu.VMEM((N_MP, STATS, ROWS), F32),
            pltpu.VMEM((ROWS, SLICE), F32),
            pltpu.VMEM((ROWS, SLICE), F32),
            pltpu.VMEM((2, EXPERTS * MSG_ROWS, ROWS), BF16),
            pltpu.VMEM((6, ROWS, EXPERTS * MSG_ROWS), BF16),
        ] + sums + sums + [
            pltpu.VMEM((EXPERTS, MSG_ROWS, MSG_LANES), BF16),
            pltpu.VMEM((N_MP, CHUNKS) + block, BF16),
            pltpu.VMEM((CHUNKS, NX) + block, BF16),
            pltpu.VMEM((CHUNKS, NX) + block, BF16),
            pltpu.VMEM((CHUNKS, NX) + block, BF16),
            pltpu.VMEM((CHUNKS, PER // 2, MSG_ROWS, MSG_LANES), BF16),
            pltpu.VMEM((CHUNKS, PER // 2, MSG_ROWS, MSG_LANES), BF16),
            pltpu.VMEM((CHUNKS,) + block, BF16),
            pltpu.VMEM((CHUNKS,) + block, BF16),
            pltpu.VMEM((CHUNKS,) + block, BF16),
            pltpu.VMEM((EXPERTS, MSG_ROWS, MSG_LANES), BF16),
            dma((len(operands),)),
            dma((5, PARTS)),
            dma((5, PARTS)),
            dma((5, PARTS)),
            dma((5, PARTS)),
            dma((11,)),
            dma((11,)),
            dma((N_MP,)),
            dma((N_MP,)),
            dma((N_MP,)),
            dma((N_MP,)),
            dma,
            dma((CHUNKS,)),
            dma((8, CHUNKS)),
            dma((8, CHUNKS)),
            dma((5, CHUNKS)),
            dma((5, CHUNKS)),
            dma,
            dma,
        ],
        compiler_params=pltpu.CompilerParams(
            collective_id=1, has_side_effects=True, vmem_limit_bytes=VMEM_LIMIT
        ),
        name="whole",
    )(*operands)


def local(
    enc_context, enc_resid, enc_out_w, final_gain, kv_weight, img_queries, img_resid, dec_out_w,
    moe_gain, router_w, expert_ids, text_lengths, expert_in, expert_out,
):
    return call(
        enc_context, enc_out_w, enc_resid, final_gain, kv_weight, router_w.T, expert_ids.T, img_queries, img_resid,
        moe_gain, text_lengths, dec_out_w, expert_in[0], expert_out[0],
    )


def solution(mesh):
    placed = (
        P("dp", "mp"),
        P("dp", "mp"),
        P("mp", None),
        P("mp"),
        P(None, None, "mp"),
        P("dp", "mp"),
        P("dp", "mp"),
        P("mp", None),
        P("mp"),
        P("mp", None),
        P("dp", None),
        P("dp"),
        P("dp", None, "mp"),
        P("dp", "mp", None),
    )
    return jax.shard_map(
        local, mesh=mesh, in_specs=placed, out_specs=(P("dp", "mp"), P("dp", "mp")), check_vma=False
    )
```

time: 251 us -> 122 us (0.49); the launches traced: 247 us -> 121 us
  waiting for transfers between devices: 93 us -> 0 us
  blocking collectives: 39.3 us -> 0 us
  Pallas kernels: 80.1 us -> 117 us
  between operations: 14.5 us -> 1.29 us
  matrix products: 10.3 us -> 0 us
  other arithmetic: 3.92 us -> 0 us
  local copies, waits for them, and re-layouts: 6.14 us -> 3.14 us
    reduce_scatter x2 -> x0, waiting for transfers between devices: 68.1 us -> none  [the longest x1 36.9 us: local(): lax.psum_scatter(text_part, 'mp', scatter_dimension=1, tiled=True)]
    psum x2 -> x0, blocking collectives: 39.3 us -> none  [the longest x1 24.4 us: local(): stats = lax.psum(part, 'mp')]
    pallas_call x1, Pallas kernels: 80.1 us -> 117 us  [call(): pl.pallas_call(kernel, out_shape=(jax.ShapeDtypeStruct((ROWS, SLICE), BF1...]
    all_gather x1 -> x0, waiting for transfers between devices: 24.9 us -> none  [local(): lax.all_gather(encoded, 'mp', axis=1, tiled=True)]
    dot_general x6 -> x0, matrix products: 10 us -> none  [the longest x1 3.42 us: local(): cross_part = jnp.dot(context, dec_out_w, preferred_element_type=jnp.float32)]
    unnamed x21 -> x2, local copies, waits for them, and re-layouts: 5.23 us -> 3.14 us
  transfers between devices with their start and end apart: 3 -> 0, of which waited for: 3 -> 0; matrix products, arithmetic and copies ran while one was open for 1% -> 0% of each run, Pallas kernels for 0% -> 0%
where the time goes in v2:
time: 122 us; the launch traced here: 121 us
  Pallas kernels  117 us (96%)
  local copies, waits for them, and re-layouts  3.14 us (3%)
  between operations  1.29 us (1%)
    pallas_call x1, Pallas kernels, call(): pl.pallas_call(kernel, out_shape=(jax.ShapeDtypeStruct((ROWS, SLICE), BF1...  117 us
    unnamed x2, local copies, waits for them, and re-layouts  3.14 us

profile of v2, /device:TPU:1, one launch (start us, length us, event | category | flops | bytes accessed | tf_op | source)
XLA Modules:
  0.0 121.1 jit_solution(8178911648366182412)
XLA Ops:
  1.3 116.7 %whole.1 = (bf16[128,512]{1,0:T(8,128)(2,1)}, bf16[128,512]{1,0:T(8,128)(2,1)}) custom-call(bf16[128,256]{1,0:T(8,128)(2,1)} %refs_0_.1, bf16[256,4096]{1,0:T(8,128)(2,1)} %refs_1_.1, bf16[128,512]{1,0:T(8,128)(2,1)} %refs_2_.1, bf16[512]{0:T(512)(128)(2,1)} %refs_3_.1, bf16[2,4096,256]{2,1,0:T(8,128)(2,1)} %refs_4_.1, bf16[32,512]{1,0:T(8,128)(2,1)} %bitcast.6, ...), custom_call_target="tpu_custom_call" | custom-call | tf_op jit(solution)/shard_map/whole/pallas_call | solution.py:540
  118.0 1.6 %copy.19 = bf16[128,512]{1,0:T(8,128)(2,1)} copy(bf16[128,512]{1,0:T(8,128)(2,1)} %get-tuple-element.4) | data formatting | bytes 262144
  119.6 1.6 %copy.20 = bf16[128,512]{1,0:T(8,128)(2,1)} copy(bf16[128,512]{1,0:T(8,128)(2,1)} %get-tuple-element.5) | data formatting | bytes 262144

commit v3 on v2

--- a/solution.py
+++ b/solution.py
@@ -17,9 +17,9 @@
 SLICE = WIDTH // N_MP
 ROWS = 128
 FF_SLICE = 256
-MSG_ROWS, MSG_LANES = 16, 768
+MSG_ROWS, MSG_LANES, CAP = 16, 768, 24
 HALF = SLICE // 2
-CHUNKS = 8
+CHUNKS = 16
 PER = N_DP // CHUNKS
 F32, BF16 = jnp.float32, jnp.bfloat16
 VMEM_LIMIT = 56 * 2**20
@@ -32,19 +32,20 @@
 
 
 def offset_of(order):
-    turn, place = order // PER, order % PER
+    turn, place = order // 4, order % 4
     kind, odd = turn % 2, place % 2
     reach = 1 + kind + 2 * (place // 2)
     dz = ((1 - odd) * reach + odd * (NZ - reach)) * (1 - kind * (place // 3))
     return dz, turn // 2
 
 
+SPREAD = FF_SLICE // 2
 PARTS = 2
 PART = ROWS // PARTS
 STATS = 40
-AHEAD = 3
+AHEAD = 6
 SELF = 7
-LAGS = (0, 1, 2, 3, 4, 5, 6)
+LAGS = (0, 3, 4, 7, 10, 11, 14)
 
 
 def kernel(*refs):
@@ -54,12 +55,13 @@
         enc_context, enc_w, enc_resid, final_gain, kv_w, router, ids_row, img_queries, img_resid, moe_gain,
         lengths, dec_w, w_in, w_out,
         state, gathered, squares, tables, hidden, router_wide, picks, gated,
-        enc_give, enc_kept, enc_taken, enc_half_l, enc_half_r, enc_sum_l, enc_sum_r,
-        dec_give, dec_kept, dec_taken, dec_half_l, dec_half_r, dec_sum_l, dec_sum_r,
-        packed, full, give, kept, taken, half_l, half_r, sum_l, sum_r, done, back,
+        enc_give, enc_kept, enc_taken, enc_sum_f, enc_sum_l, enc_sum_r,
+        dec_give, dec_kept, dec_taken, dec_sum_f, dec_sum_l, dec_sum_r,
+        packed, full, part_out, part_in, part_own, inner, last_out, last_in, last_own, done, back,
         load_sem, enc_send, enc_recv, dec_send, dec_recv, ag_send, ag_recv,
         square_send, square_recv, table_send, table_recv,
-        disp_send, disp_recv, slot_send, slot_recv, rs_send, rs_recv, ret_send, ret_recv,
+        disp_send, disp_recv, slot_send, slot_recv, inner_send, inner_recv, cross_send, cross_recv,
+        in_send, in_recv, out_send, out_recv, ret_send, ret_recv,
     ) = rest
     targets = rest[2:16]
     dp, mp = lax.axis_index("dp"), lax.axis_index("mp")
@@ -67,7 +69,7 @@
     x, core = mp // 2, mp % 2
     x_right, x_left, x_far = (x + 1) % NX, (x + NX - 1) % NX, (x + 2) % NX
     m_right, m_left, m_far = x_right * 2 + core, x_left * 2 + core, x_far * 2 + core
-    sibling, right, left = (dp, x * 2 + 1 - core), (dp, m_right), (dp, m_left)
+    sibling, right, left, far = (dp, x * 2 + 1 - core), (dp, m_right), (dp, m_left), (dp, m_far)
 
     def dest_of(order):
         dz, dy = offset_of(order)
@@ -79,8 +81,57 @@
 
     loads = [
         pltpu.make_async_copy(src, dst, load_sem.at[i])
-        for i, (src, dst) in enumerate(zip(sources, targets))
+        for i, (src, dst) in enumerate(zip(sources[:-2], targets))
     ]
+    w_in_hbm, w_out_hbm = sources[-2:]
+
+    x_a, x_b = NX - 1 - x, x + 1 - 2 * (x % 2)
+    m_a, m_b, m_sib = x_a * 2 + core, x_b * 2 + core, x * 2 + 1 - core
+    m_a_sib = x_a * 2 + 1 - core
+    pair_a, pair_b = (dp, m_a), (dp, m_b)
+    chip = 2 * SLICE
+
+    def in_rows(of, start, count):
+        return w_in_hbm.at[pl.ds(pl.multiple_of(of * chip + start, 128), count)]
+
+    def out_block(part, m):
+        return w_out_hbm.at[pl.ds(part * SPREAD, SPREAD), pl.ds(pl.multiple_of(m * SLICE, SLICE), SLICE)]
+
+    def out_whole(m):
+        return w_out_hbm.at[:, pl.ds(pl.multiple_of(m * SLICE, SLICE), SLICE)]
+
+    count = len(sources)
+    loads += [
+        pltpu.make_async_copy(in_rows(x, 0, chip), w_in.at[0, pl.ds(0, chip)], load_sem.at[count - 2]),
+        pltpu.make_async_copy(in_rows(x_a, 0, chip), w_in.at[0, pl.ds(chip, chip)], load_sem.at[count - 1]),
+        pltpu.make_async_copy(out_whole(mp), w_out.at[0, 0], load_sem.at[count]),
+        pltpu.make_async_copy(out_whole(m_b), w_out.at[0, 1], load_sem.at[count + 1]),
+    ]
+
+    def in_copy(piece):
+        side, start = piece // 4, piece % 4 * FF_SLICE
+        of = x_b if side == 0 else NX - 1 - x_b
+        return remote(
+            in_rows(of, start, FF_SLICE), w_in.at[1, pl.ds(side * chip + start, FF_SLICE)],
+            in_send.at[piece], in_recv.at[piece], pair_b,
+        )
+
+    def out_copy(kind, piece):
+        to = (m_sib, m_a, m_a_sib)[kind]
+        which, part = piece // 2, piece % 2
+        to_chip = to // 2
+        m = to if which == 0 else (to_chip + 1 - 2 * (to_chip % 2)) * 2 + to % 2
+        return remote(
+            out_block(part, m), w_out.at[kind + 1, which, pl.ds(part * SPREAD, SPREAD)],
+            out_send.at[kind, piece], out_recv.at[kind, piece], (dp, to),
+        )
+
+    def spread(ins, outs):
+        for piece in ins:
+            in_copy(piece).start()
+        for unit in outs:
+            out_copy(1 + unit % 2, unit // 2).start()
+
     for load in loads[:3]:
         load.start()
     barrier = pltpu.get_barrier_semaphore()
@@ -96,16 +147,13 @@
     for load in loads[3:]:
         load.start()
 
-    def reduce_scatter(values, weights, resid, out, give, kept, taken, half_l, half_r, sum_l, sum_r, send, recv):
-        half = PART // 2
-
+    def reduce_scatter(values, weights, resid, out, give, kept, taken, sum_f, sum_l, sum_r, send, recv):
         def copy(kind, r):
             src, dst, device = {
                 0: (give.at[r], taken.at[r], sibling),
-                1: (kept.at[r, x_far, pl.ds(0, half)], half_l.at[r], right),
-                2: (kept.at[r, x_far, pl.ds(half, half)], half_r.at[r], left),
-                3: (kept.at[r, x_right], sum_l.at[r], right),
-                4: (kept.at[r, x_left], sum_r.at[r], left),
+                1: (kept.at[r, x_far], sum_f.at[r], far),
+                2: (kept.at[r, x_right], sum_l.at[r], right),
+                3: (kept.at[r, x_left], sum_r.at[r], left),
             }[kind]
             return remote(src, dst, send.at[kind, r], recv.at[kind, r], device)
 
@@ -124,35 +172,33 @@
             if r == 0 and out is state:
                 pl.semaphore_wait(barrier, N_MP - 1 + N_DP - 1)
             copy(0, r).start()
+            if r == 0 and out is state:
+                spread((0,), (0,))
+                for piece in range(4):
+                    out_copy(0, piece).start()
         for r in range(PARTS):
             for px in range(NX):
                 product(kept, r, px, core)
         for r in range(PARTS):
             copy(0, r).wait_recv()
-            kept[r, x_far] = pair(r, x_far).astype(BF16)
-            copy(1, r).start()
-            copy(2, r).start()
-        first, second = slice(0, half), slice(half, PART)
-        for r in range(PARTS):
-            copy(1, r).wait_recv()
-            kept[r, x_right, first] = (pair(r, x_right, first) + half_l[r].astype(F32)).astype(BF16)
-            kept[r, x_right, second] = pair(r, x_right, second).astype(BF16)
-            copy(3, r).start()
-            copy(2, r).wait_recv()
-            kept[r, x_left, first] = pair(r, x_left, first).astype(BF16)
-            kept[r, x_left, second] = (pair(r, x_left, second) + half_r[r].astype(F32)).astype(BF16)
-            copy(4, r).start()
+            for kind, px in ((1, x_far), (2, x_right), (3, x_left)):
+                kept[r, px] = pair(r, px).astype(BF16)
+                copy(kind, r).start()
+        if out is state:
+            pass
+        else:
+            pass
         for r in range(PARTS):
             rows = slice(r * PART, (r + 1) * PART)
             base = resid[rows].astype(F32) + pair(r, x)
-            copy(3, r).wait_recv()
-            copy(4, r).wait_recv()
-            out[rows] = base + sum_l[r].astype(F32) + sum_r[r].astype(F32)
+            for kind in (2, 3, 1):
+                copy(kind, r).wait_recv()
+            out[rows] = base + sum_l[r].astype(F32) + sum_r[r].astype(F32) + sum_f[r].astype(F32)
             yield r
 
         def drain():
             for r in range(PARTS):
-                for kind in range(5):
+                for kind in range(4):
                     copy(kind, r).wait_send()
 
         drains.append(drain)
@@ -179,7 +225,7 @@
             0: (gathered.at[mp, 0], sibling), 1: (gathered.at[mp, 1], sibling),
             2: (gathered.at[mp, 0], right), 3: (gathered.at[mp, 1], right),
             4: (gathered.at[mp, 0], left), 5: (gathered.at[mp, 1], left),
-            6: (gathered.at[m_left, 0], right), 7: (gathered.at[m_right, 1], left),
+            6: (gathered.at[mp, 0], far), 7: (gathered.at[mp, 1], far),
             8: (gathered.at[m_left], sibling), 9: (gathered.at[m_right], sibling),
             10: (gathered.at[m_far], sibling),
         }[kind]
@@ -189,12 +235,13 @@
         load.wait()
     text_gain = final_gain[...].astype(F32).reshape(1, SLICE)
     for r in reduce_scatter(
-        enc_context[...], enc_w, enc_resid, state, enc_give, enc_kept, enc_taken, enc_half_l, enc_half_r,
+        enc_context[...], enc_w, enc_resid, state, enc_give, enc_kept, enc_taken, enc_sum_f,
         enc_sum_l, enc_sum_r, enc_send, enc_recv,
     ):
         gathered[mp, r] = (state[r * PART:(r + 1) * PART] * text_gain).astype(BF16)
-        for kind in ((2, 4, 0), (5, 3, 1))[r]:
+        for kind in ((6, 2, 4, 0), (7, 3, 5, 1))[r]:
             gather_copy(kind).start()
+    pass
     text_state = state[...]
     square = jnp.sum(text_state * text_state, axis=1, keepdims=True)
     squares[mp] = jnp.transpose(jnp.broadcast_to(square, (ROWS, ROWS)))[0:8]
@@ -245,22 +292,16 @@
             )
 
     project(mp)
-    gather_copy(2).wait_recv()
-    gather_copy(6).start()
-    gather_copy(5).wait_recv()
-    gather_copy(7).start()
-    gather_copy(3).wait_recv()
-    gather_copy(8).start()
-    gather_copy(4).wait_recv()
-    gather_copy(9).start()
+    for kinds, on in (((2, 3), 8), ((4, 5), 9), ((6, 7), 10)):
+        for kind in kinds:
+            gather_copy(kind).wait_recv()
+        gather_copy(on).start()
+    spread((1, 2, 3, 4), (1, 2, 3, 4))
     project(m_left)
     project(m_right)
     gather_copy(0).wait_recv()
     gather_copy(1).wait_recv()
     project(x * 2 + 1 - core)
-    gather_copy(6).wait_recv()
-    gather_copy(7).wait_recv()
-    gather_copy(10).start()
     project(m_far)
     for kind, px in ((8, x_left), (9, x_right), (10, x_far)):
         gather_copy(kind).wait_recv()
@@ -293,7 +334,7 @@
     context = context.astype(BF16)
 
     for _ in reduce_scatter(
-        context, dec_w, img_resid, hidden, dec_give, dec_kept, dec_taken, dec_half_l, dec_half_r,
+        context, dec_w, img_resid, hidden, dec_give, dec_kept, dec_taken, dec_sum_f,
         dec_sum_l, dec_sum_r, dec_send, dec_recv,
     ):
         pass
@@ -306,7 +347,9 @@
     )
     lane = lax.broadcasted_iota(jnp.int32, (ROWS, ROWS), 1)
     tables[mp] = jnp.transpose(jnp.where(lane == EXPERTS, square, logits))[0:STATS]
-    exchange(tables, table_send, table_recv)()
+    tables_done = exchange(tables, table_send, table_recv)
+    spread((5, 6, 7), (5, 6, 7))
+    tables_done()
     total = tables[0]
     for m in range(1, N_MP):
         total = total + tables[m]
@@ -357,27 +400,16 @@
         gated[2 * i] = main
         gated[2 * i + 1] = (weights - main.astype(F32)).astype(BF16)
 
-    half = PER // 2
-
-    def slot_copy(kind, k):
-        src = {
-            0: (mp, None, sibling), 1: (mp, None, right), 2: (mp, None, left),
-            3: (m_left, 0, right), 4: (m_right, half, left),
-            5: (m_left, None, sibling), 6: (m_right, None, sibling), 7: (m_far, None, sibling),
-        }[kind]
-        place, part, device = src
-        ref = full.at[place, k] if part is None else full.at[place, k, pl.ds(part, half)]
-        return remote(ref, ref, slot_send.at[kind, k], slot_recv.at[kind, k], device)
-
-    def sum_copy(kind, k):
-        src, dst, device = {
-            0: (give.at[k], taken.at[k], sibling),
-            1: (kept.at[k, x_far, pl.ds(0, half)], half_l.at[k], right),
-            2: (kept.at[k, x_far, pl.ds(half, half)], half_r.at[k], left),
-            3: (kept.at[k, x_right], sum_l.at[k], right),
-            4: (kept.at[k, x_left], sum_r.at[k], left),
-        }[kind]
-        return remote(src, dst, rs_send.at[kind, k], rs_recv.at[kind, k], device)
+    def shared_copy(ref, send, recv, kind, k):
+        place, device = ((mp, sibling), (mp, pair_a), (m_a, sibling))[kind]
+        return remote(ref.at[place, k], ref.at[place, k], send.at[kind, k], recv.at[kind, k], device)
+
+    slot_copy = functools.partial(shared_copy, full, slot_send, slot_recv)
+    inner_copy = functools.partial(shared_copy, inner, inner_send, inner_recv)
+
+    def cross_copy(kind, k):
+        src, dst = ((part_out, part_in), (last_out, last_in))[kind]
+        return remote(src.at[k], dst.at[k], cross_send.at[kind, k], cross_recv.at[kind, k], pair_b)
 
     def arrive(k):
         @pl.when(k + AHEAD < CHUNKS)
@@ -386,87 +418,84 @@
             lax.fori_loop(first, first + PER, dispatch, 0)
 
         pltpu.make_async_copy(full.at[mp, k], full.at[mp, k], disp_recv.at[k]).wait()
-        for kind in (1, 2, 0):
+        for kind in (1, 0):
             slot_copy(kind, k).start()
 
-    def forward(k):
-        slot_copy(1, k).wait_recv()
-        slot_copy(3, k).start()
+    def forward(copy, k):
+        copy(1, k).wait_recv()
+        copy(2, k).start()
+
+    rows = PER * MSG_ROWS
+
+    def first_product(k):
+        @pl.when(k == 0)
+        def _():
+            for piece in range(8):
+                in_copy(piece).wait_recv()
+
+        slot_copy(0, k).wait_recv()
         slot_copy(2, k).wait_recv()
-        slot_copy(4, k).start()
-        slot_copy(5, k).start()
-        slot_copy(6, k).start()
-
-    def forward_far(k):
-        slot_copy(3, k).wait_recv()
-        slot_copy(4, k).wait_recv()
-        slot_copy(7, k).start()
-
-    def compute(k):
-        for kind in (0, 5, 6, 7):
-            slot_copy(kind, k).wait_recv()
-
-        rows = PER * MSG_ROWS
-        low = jnp.zeros((2 * rows, FF_SLICE), F32)
-        high = jnp.zeros((2 * rows, FF_SLICE), F32)
-        for s in range(N_MP):
-            block = full[s, k].reshape(rows, MSG_LANES)
-            end = block[:, SLICE:]
-            low = low + jnp.dot(
-                jnp.concatenate([block[:, 0:HALF], end], axis=0),
-                w_in[s * SLICE:s * SLICE + HALF, :],
-                preferred_element_type=F32,
+        order = (x * 2, x * 2 + 1, x_a * 2, x_a * 2 + 1)
+
+        def product(side):
+            low = jnp.zeros((2 * rows, FF_SLICE), F32)
+            high = jnp.zeros((2 * rows, FF_SLICE), F32)
+            for j, m in enumerate(order):
+                block = full[m, k].reshape(rows, MSG_LANES)
+                end = block[:, SLICE:]
+                low = low + jnp.dot(
+                    jnp.concatenate([block[:, 0:HALF], end], axis=0),
+                    w_in[side, j * SLICE:j * SLICE + HALF],
+                    preferred_element_type=F32,
+                )
+                high = high + jnp.dot(
+                    jnp.concatenate([block[:, HALF:SLICE], end], axis=0),
+                    w_in[side, j * SLICE + HALF:(j + 1) * SLICE],
+                    preferred_element_type=F32,
+                )
+            ends = (
+                low[rows:].reshape(PER, MSG_ROWS, FF_SLICE)[:, 0:8]
+                + high[rows:].reshape(PER, MSG_ROWS, FF_SLICE)[:, 8:16]
             )
-            high = high + jnp.dot(
-                jnp.concatenate([block[:, HALF:SLICE], end], axis=0),
-                w_in[s * SLICE + HALF:(s + 1) * SLICE, :],
-                preferred_element_type=F32,
-            )
-        ends = (
-            low[rows:].reshape(PER, MSG_ROWS, FF_SLICE)[:, 0:8]
-            + high[rows:].reshape(PER, MSG_ROWS, FF_SLICE)[:, 8:16]
-        )
-        before = jnp.concatenate([low[:rows] + high[:rows], ends.reshape(PER * 8, FF_SLICE)], axis=0)
-        inner = jax.nn.gelu(before, approximate=True).astype(BF16)
-
-        def result(ref, px, side):
-            at = pl.multiple_of((px * 2 + side) * SLICE, SLICE)
-            out = jnp.dot(inner, w_out[:, pl.ds(at, SLICE)], preferred_element_type=F32)
-            ref[k, px, :, :, 0:SLICE] = out[:rows].astype(BF16).reshape(PER, MSG_ROWS, SLICE)
+            return jnp.concatenate([low[:rows] + high[:rows], ends.reshape(PER * 8, FF_SLICE)], axis=0)
+
+        part_out[k] = product(1).astype(BF16)
+        cross_copy(0, k).start()
+        part_own[k] = product(0)
+
+    def activate(k):
+        cross_copy(0, k).wait_recv()
+        before = part_own[k] + part_in[k].astype(F32)
+        inner[mp, k] = jax.nn.gelu(before, approximate=True).astype(BF16)
+        for kind in (1, 0):
+            inner_copy(kind, k).start()
+
+    def second_product(k):
+        @pl.when(k == 0)
+        def _():
+            for kind in range(3):
+                for piece in range(4):
+                    out_copy(kind, piece).wait_recv()
+
+        inner_copy(0, k).wait_recv()
+        inner_copy(2, k).wait_recv()
+
+        def product(ref, which):
+            out = jnp.zeros((PER * CAP, SLICE), F32)
+            for j, m in enumerate((mp, m_sib, m_a, m_a_sib)):
+                out = out + jnp.dot(inner[m, k], w_out[j, which], preferred_element_type=F32)
+            ref[k, :, :, 0:SLICE] = out[:rows].astype(ref.dtype).reshape(PER, MSG_ROWS, SLICE)
             ends = out[rows:].reshape(PER, 8, SLICE)
             ends = jnp.concatenate([ends[:, :, 0:HALF], ends[:, :, HALF:SLICE]], axis=1)
-            ref[k, px, :, :, SLICE:MSG_LANES] = ends.astype(BF16)
-
-        for px in range(NX):
-            result(give, px, 1 - core)
-        sum_copy(0, k).start()
-        for px in range(NX):
-            result(kept, px, core)
-
-    def pair(k, px, part=slice(None)):
-        return kept[k, px, part].astype(F32) + taken[k, px, part].astype(F32)
-
-    def add_sibling(k):
-        sum_copy(0, k).wait_recv()
-        kept[k, x_far] = pair(k, x_far).astype(BF16)
-        sum_copy(1, k).start()
-        sum_copy(2, k).start()
-
-    def add_far(k):
-        first, second = slice(0, half), slice(half, PER)
-        sum_copy(1, k).wait_recv()
-        kept[k, x_right, first] = (pair(k, x_right, first) + half_l[k].astype(F32)).astype(BF16)
-        kept[k, x_right, second] = pair(k, x_right, second).astype(BF16)
-        sum_copy(3, k).start()
-        sum_copy(2, k).wait_recv()
-        kept[k, x_left, first] = pair(k, x_left, first).astype(BF16)
-        kept[k, x_left, second] = (pair(k, x_left, second) + half_r[k].astype(F32)).astype(BF16)
-        sum_copy(4, k).start()
+            ref[k, :, :, SLICE:MSG_LANES] = ends.astype(ref.dtype)
+
+        product(last_out, 1)
+        cross_copy(1, k).start()
+        product(last_own, 0)
 
     def finish(k):
-        sum_copy(3, k).wait_recv()
-        sum_copy(4, k).wait_recv()
-        done[k] = (pair(k, x) + sum_l[k].astype(F32) + sum_r[k].astype(F32)).astype(BF16)
+        cross_copy(1, k).wait_recv()
+        done[k] = (last_own[k] + last_in[k].astype(F32)).astype(BF16)
         for j in range(PER):
             order = k * PER + j
             origin = origin_of(order)
@@ -480,12 +509,16 @@
                     remote(done.at[k, j], back.at[dp], ret_send, ret_recv, (origin, mp)).start()
             else:
                 remote(done.at[k, j], back.at[dp], ret_send, ret_recv, (origin, mp)).start()
-        for kind in range(8):
+        for kind in range(3):
             slot_copy(kind, k).wait_send()
-        for kind in range(5):
-            sum_copy(kind, k).wait_send()
-
-    stages = (arrive, forward, forward_far, compute, add_sibling, add_far, finish)
+            inner_copy(kind, k).wait_send()
+        for kind in range(2):
+            cross_copy(kind, k).wait_send()
+
+    stages = (
+        arrive, functools.partial(forward, slot_copy), first_product, activate,
+        functools.partial(forward, inner_copy), second_product, finish,
+    )
 
     def step(i, carry):
         for lag, stage in zip(LAGS, stages):
@@ -518,6 +551,11 @@
         drain()
     for kind in range(11):
         gather_copy(kind).wait_send()
+    for piece in range(8):
+        in_copy(piece).wait_send()
+    for kind in range(3):
+        for piece in range(4):
+            out_copy(kind, piece).wait_send()
 
 
 def call(*operands):
@@ -529,14 +567,13 @@
         pltpu.VMEM((PARTS, NX, PART, SLICE), BF16),
         pltpu.VMEM((PARTS, NX, PART, SLICE), BF16),
         pltpu.VMEM((PARTS, NX, PART, SLICE), BF16),
-        pltpu.VMEM((PARTS, PART // 2, SLICE), BF16),
-        pltpu.VMEM((PARTS, PART // 2, SLICE), BF16),
+        pltpu.VMEM((PARTS, PART, SLICE), BF16),
         pltpu.VMEM((PARTS, PART, SLICE), BF16),
         pltpu.VMEM((PARTS, PART, SLICE), BF16),
     ]
     landing = [
-        pltpu.SMEM(o.shape, o.dtype) if o.shape == (1,) else pltpu.VMEM(o.shape, o.dtype) for o in operands
-    ]
+        pltpu.SMEM(o.shape, o.dtype) if o.shape == (1,) else pltpu.VMEM(o.shape, o.dtype) for o in operands[:-2]
+    ] + [pltpu.VMEM((2, WIDTH // 2, FF_SLICE), BF16), pltpu.VMEM((4, 2, FF_SLICE, SLICE), BF16)]
     return pl.pallas_call(
         kernel,
         out_shape=(jax.ShapeDtypeStruct((ROWS, SLICE), BF16), jax.ShapeDtypeStruct((ROWS, SLICE), BF16)),
@@ -554,16 +591,16 @@
         ] + sums + sums + [
             pltpu.VMEM((EXPERTS, MSG_ROWS, MSG_LANES), BF16),
             pltpu.VMEM((N_MP, CHUNKS) + block, BF16),
-            pltpu.VMEM((CHUNKS, NX) + block, BF16),
-            pltpu.VMEM((CHUNKS, NX) + block, BF16),
-            pltpu.VMEM((CHUNKS, NX) + block, BF16),
-            pltpu.VMEM((CHUNKS, PER // 2, MSG_ROWS, MSG_LANES), BF16),
-            pltpu.VMEM((CHUNKS, PER // 2, MSG_ROWS, MSG_LANES), BF16),
+            pltpu.VMEM((CHUNKS, PER * CAP, FF_SLICE), BF16),
+            pltpu.VMEM((CHUNKS, PER * CAP, FF_SLICE), BF16),
+            pltpu.VMEM((CHUNKS, PER * CAP, FF_SLICE), F32),
+            pltpu.VMEM((N_MP, CHUNKS, PER * CAP, FF_SLICE), BF16),
             pltpu.VMEM((CHUNKS,) + block, BF16),
             pltpu.VMEM((CHUNKS,) + block, BF16),
+            pltpu.VMEM((CHUNKS,) + block, F32),
             pltpu.VMEM((CHUNKS,) + block, BF16),
             pltpu.VMEM((EXPERTS, MSG_ROWS, MSG_LANES), BF16),
-            dma((len(operands),)),
+            dma((len(operands) + 2,)),
             dma((5, PARTS)),
             dma((5, PARTS)),
             dma((5, PARTS)),
@@ -576,10 +613,16 @@
             dma((N_MP,)),
             dma,
             dma((CHUNKS,)),
-            dma((8, CHUNKS)),
-            dma((8, CHUNKS)),
-            dma((5, CHUNKS)),
-            dma((5, CHUNKS)),
+            dma((3, CHUNKS)),
+            dma((3, CHUNKS)),
+            dma((3, CHUNKS)),
+            dma((3, CHUNKS)),
+            dma((2, CHUNKS)),
+            dma((2, CHUNKS)),
+            dma((8,)),
+            dma((8,)),
+            dma((3, 4)),
+            dma((3, 4)),
             dma,
             dma,
         ],

time: 122 us -> 112 us (0.918)
  Pallas kernels: 117 us -> 107 us
    pallas_call x1, Pallas kernels: 117 us -> 107 us  [call(): pl.pallas_call(kernel, out_shape=(jax.ShapeDtypeStruct((ROWS, SLICE), BF1...]
where the time goes in v3:
time: 112 us
  Pallas kernels  107 us (96%)
  local copies, waits for them, and re-layouts  3.14 us (3%)
  between operations  1.29 us (1%)
    pallas_call x1, Pallas kernels, call(): pl.pallas_call(kernel, out_shape=(jax.ShapeDtypeStruct((ROWS, SLICE), BF1...  107 us
    unnamed x2, local copies, waits for them, and re-layouts  3.14 us

profile of v3, /device:TPU:1, one launch (start us, length us, event | category | flops | bytes accessed | tf_op | source)
XLA Modules:
  0.0 111.9 jit_solution(11891263031444340550)
XLA Ops:
  1.3 107.4 %whole.1 = (bf16[128,512]{1,0:T(8,128)(2,1)}, bf16[128,512]{1,0:T(8,128)(2,1)}) custom-call(bf16[128,256]{1,0:T(8,128)(2,1)} %refs_0_.1, bf16[256,4096]{1,0:T(8,128)(2,1)} %refs_1_.1, bf16[128,512]{1,0:T(8,128)(2,1)} %refs_2_.1, bf16[512]{0:T(512)(128)(2,1)} %refs_3_.1, bf16[2,4096,256]{2,1,0:T(8,128)(2,1)} %refs_4_.1, bf16[32,512]{1,0:T(8,128)(2,1)} %bitcast.6, ...), custom_call_target="tpu_custom_call" | custom-call | tf_op jit(solution)/shard_map/whole/pallas_call | solution.py:577
  108.7 1.6 %copy.19 = bf16[128,512]{1,0:T(8,128)(2,1)} copy(bf16[128,512]{1,0:T(8,128)(2,1)} %get-tuple-element.4) | data formatting | bytes 262144
  110.3 1.6 %copy.20 = bf16[128,512]{1,0:T(8,128)(2,1)} copy(bf16[128,512]{1,0:T(8,128)(2,1)} %get-tuple-element.5) | data formatting | bytes 262144

commit v4 on v3

--- a/solution.py
+++ b/solution.py
@@ -32,11 +32,13 @@
 
 
 def offset_of(order):
-    turn, place = order // 4, order % 4
-    kind, odd = turn % 2, place % 2
+    high, place = order // 16, order % 8
+    place = (1 - high) * place + high * (7 - place)
+    kind, place = place // 4, place % 4
+    odd = place % 2
     reach = 1 + kind + 2 * (place // 2)
     dz = ((1 - odd) * reach + odd * (NZ - reach)) * (1 - kind * (place // 3))
-    return dz, turn // 2
+    return dz, order // 8
 
 
 SPREAD = FF_SLICE // 2
@@ -45,7 +47,7 @@
 STATS = 40
 AHEAD = 6
 SELF = 7
-LAGS = (0, 3, 4, 7, 10, 11, 14)
+LAGS = (0, 3, 4, 6, 9, 10, 13)
 
 
 def kernel(*refs):
@@ -296,7 +298,7 @@
         for kind in kinds:
             gather_copy(kind).wait_recv()
         gather_copy(on).start()
-    spread((1, 2, 3, 4), (1, 2, 3, 4))
+    spread((1, 2, 3), (1, 2, 3))
     project(m_left)
     project(m_right)
     gather_copy(0).wait_recv()
@@ -348,7 +350,7 @@
     lane = lax.broadcasted_iota(jnp.int32, (ROWS, ROWS), 1)
     tables[mp] = jnp.transpose(jnp.where(lane == EXPERTS, square, logits))[0:STATS]
     tables_done = exchange(tables, table_send, table_recv)
-    spread((5, 6, 7), (5, 6, 7))
+    spread((4, 5, 6, 7), (4, 5, 6, 7))
     tables_done()
     total = tables[0]
     for m in range(1, N_MP):
@@ -529,24 +531,6 @@
 
     lax.fori_loop(0, CHUNKS + LAGS[-1], step, 0)
 
-    pltpu.make_async_copy(back, back, ret_recv).wait()
-
-    def weigh(i, values):
-        return jnp.dot(gated[2 * i], values, preferred_element_type=F32) + jnp.dot(
-            gated[2 * i + 1], values, preferred_element_type=F32
-        )
-
-    results = back[...].reshape(EXPERTS * MSG_ROWS, MSG_LANES)
-    ends = results[:, SLICE:]
-    moe = weigh(0, results[:, 0:SLICE])
-    mixed[:, 0:HALF] = (hidden[:, 0:HALF] + moe[:, 0:HALF] + weigh(1, ends)).astype(BF16)
-    mixed[:, HALF:] = (hidden[:, HALF:] + moe[:, HALF:] + weigh(2, ends)).astype(BF16)
-
-    most = packed.at[pl.ds(0, N_DP - 1)]
-    remote(most, most, disp_send, disp_recv.at[0], sibling).wait_send()
-    remote(most, most, ret_send, ret_recv, sibling).wait_send()
-
-
     for drain in drains:
         drain()
     for kind in range(11):
@@ -556,6 +540,23 @@
     for kind in range(3):
         for piece in range(4):
             out_copy(kind, piece).wait_send()
+
+    pltpu.make_async_copy(back, back, ret_recv).wait()
+
+    def weigh(i, values):
+        return jnp.dot(gated[2 * i], values, preferred_element_type=F32) + jnp.dot(
+            gated[2 * i + 1], values, preferred_element_type=F32
+        )
+
+    results = back[...].reshape(EXPERTS * MSG_ROWS, MSG_LANES)
+    ends = results[:, SLICE:]
+    moe = weigh(0, results[:, 0:SLICE])
+    mixed[:, 0:HALF] = (hidden[:, 0:HALF] + moe[:, 0:HALF] + weigh(1, ends)).astype(BF16)
+    mixed[:, HALF:] = (hidden[:, HALF:] + moe[:, HALF:] + weigh(2, ends)).astype(BF16)
+
+    most = packed.at[pl.ds(0, N_DP - 1)]
+    remote(most, most, disp_send, disp_recv.at[0], sibling).wait_send()
+    remote(most, most, ret_send, ret_recv, sibling).wait_send()
 
 
 def call(*operands):

time: 112 us -> 109 us (0.973)
  Pallas kernels: 107 us -> 105 us
    pallas_call x1, Pallas kernels: 107 us -> 105 us  [call(): pl.pallas_call(kernel, out_shape=(jax.ShapeDtypeStruct((ROWS, SLICE), BF1...]
where the time goes in v4:
time: 109 us
  Pallas kernels  105 us (96%)
  local copies, waits for them, and re-layouts  3.14 us (3%)
  between operations  1.29 us (1%)
    pallas_call x1, Pallas kernels, call(): pl.pallas_call(kernel, out_shape=(jax.ShapeDtypeStruct((ROWS, SLICE), BF1...  105 us
    unnamed x2, local copies, waits for them, and re-layouts  3.14 us

profile of v4, /device:TPU:1, one launch (start us, length us, event | category | flops | bytes accessed | tf_op | source)
XLA Modules:
  0.0 109.3 jit_solution(15515198388822282813)
XLA Ops:
  1.3 104.9 %whole.1 = (bf16[128,512]{1,0:T(8,128)(2,1)}, bf16[128,512]{1,0:T(8,128)(2,1)}) custom-call(bf16[128,256]{1,0:T(8,128)(2,1)} %refs_0_.1, bf16[256,4096]{1,0:T(8,128)(2,1)} %refs_1_.1, bf16[128,512]{1,0:T(8,128)(2,1)} %refs_2_.1, bf16[512]{0:T(512)(128)(2,1)} %refs_3_.1, bf16[2,4096,256]{2,1,0:T(8,128)(2,1)} %refs_4_.1, bf16[32,512]{1,0:T(8,128)(2,1)} %bitcast.6, ...), custom_call_target="tpu_custom_call" | custom-call | tf_op jit(solution)/shard_map/whole/pallas_call | solution.py:578
  106.2 1.6 %copy.19 = bf16[128,512]{1,0:T(8,128)(2,1)} copy(bf16[128,512]{1,0:T(8,128)(2,1)} %get-tuple-element.4) | data formatting | bytes 262144
  107.8 1.6 %copy.20 = bf16[128,512]{1,0:T(8,128)(2,1)} copy(bf16[128,512]{1,0:T(8,128)(2,1)} %get-tuple-element.5) | data formatting | bytes 262144

commit v5 on v4

--- a/solution.py
+++ b/solution.py
@@ -53,7 +53,7 @@
 def kernel(*refs):
     sources, rest = refs[:14], refs[14:]
     (
-        encoded, mixed,
+        both,
         enc_context, enc_w, enc_resid, final_gain, kv_w, router, ids_row, img_queries, img_resid, moe_gain,
         lengths, dec_w, w_in, w_out,
         state, gathered, squares, tables, hidden, router_wide, picks, gated,
@@ -65,7 +65,8 @@
         disp_send, disp_recv, slot_send, slot_recv, inner_send, inner_recv, cross_send, cross_recv,
         in_send, in_recv, out_send, out_recv, ret_send, ret_recv,
     ) = rest
-    targets = rest[2:16]
+    targets = rest[1:15]
+    encoded, mixed = both.at[0], both.at[1]
     dp, mp = lax.axis_index("dp"), lax.axis_index("mp")
     z, y = dp // NY, dp % NY
     x, core = mp // 2, mp % 2
@@ -129,9 +130,8 @@
         )
 
     def spread(ins, outs):
-        for piece in ins:
+        for piece, unit in zip(ins, outs):
             in_copy(piece).start()
-        for unit in outs:
             out_copy(1 + unit % 2, unit // 2).start()
 
     for load in loads[:3]:
@@ -186,10 +186,6 @@
             for kind, px in ((1, x_far), (2, x_right), (3, x_left)):
                 kept[r, px] = pair(r, px).astype(BF16)
                 copy(kind, r).start()
-        if out is state:
-            pass
-        else:
-            pass
         for r in range(PARTS):
             rows = slice(r * PART, (r + 1) * PART)
             base = resid[rows].astype(F32) + pair(r, x)
@@ -243,7 +239,6 @@
         gathered[mp, r] = (state[r * PART:(r + 1) * PART] * text_gain).astype(BF16)
         for kind in ((6, 2, 4, 0), (7, 3, 5, 1))[r]:
             gather_copy(kind).start()
-    pass
     text_state = state[...]
     square = jnp.sum(text_state * text_state, axis=1, keepdims=True)
     squares[mp] = jnp.transpose(jnp.broadcast_to(square, (ROWS, ROWS)))[0:8]
@@ -577,9 +572,9 @@
     ] + [pltpu.VMEM((2, WIDTH // 2, FF_SLICE), BF16), pltpu.VMEM((4, 2, FF_SLICE, SLICE), BF16)]
     return pl.pallas_call(
         kernel,
-        out_shape=(jax.ShapeDtypeStruct((ROWS, SLICE), BF16), jax.ShapeDtypeStruct((ROWS, SLICE), BF16)),
+        out_shape=jax.ShapeDtypeStruct((2, ROWS, SLICE), BF16),
         in_specs=[hbm] * len(operands),
-        out_specs=(vmem, vmem),
+        out_specs=vmem,
         scratch_shapes=landing + [
             pltpu.VMEM((ROWS, SLICE), F32),
             pltpu.VMEM((N_MP, PARTS, PART, SLICE), BF16),
@@ -638,10 +633,11 @@
     enc_context, enc_resid, enc_out_w, final_gain, kv_weight, img_queries, img_resid, dec_out_w,
     moe_gain, router_w, expert_ids, text_lengths, expert_in, expert_out,
 ):
-    return call(
+    both = call(
         enc_context, enc_out_w, enc_resid, final_gain, kv_weight, router_w.T, expert_ids.T, img_queries, img_resid,
         moe_gain, text_lengths, dec_out_w, expert_in[0], expert_out[0],
     )
+    return both[0], both[1]
 
 
 def solution(mesh):

time: 109 us -> 108 us (level)
  local copies, waits for them, and re-layouts: 3.14 us -> 1.68 us
    unnamed x2 -> x0, local copies, waits for them, and re-layouts: 3.14 us -> none
    squeeze x0 -> x1, local copies, waits for them, and re-layouts: none -> 1.68 us  [local(): return (both[0], both[1])]
where the time goes in v5:
time: 108 us
  Pallas kernels  105 us (97%)
  local copies, waits for them, and re-layouts  1.68 us (2%)
  between operations  1.29 us (1%)
    pallas_call x1, Pallas kernels, call(): pl.pallas_call(kernel, out_shape=jax.ShapeDtypeStruct((2, ROWS, SLICE), B...  105 us

profile of v5, /device:TPU:1, one launch (start us, length us, event | category | flops | bytes accessed | tf_op | source)
XLA Modules:
  0.0 107.9 jit_solution(1000183632571824264)
XLA Ops:
  1.3 104.9 %whole.1 = bf16[2,128,512]{2,1,0:T(8,128)(2,1)} custom-call(bf16[128,256]{1,0:T(8,128)(2,1)} %refs_0_.1, bf16[256,4096]{1,0:T(8,128)(2,1)} %refs_1_.1, bf16[128,512]{1,0:T(8,128)(2,1)} %refs_2_.1, bf16[512]{0:T(512)(128)(2,1)} %refs_3_.1, bf16[2,4096,256]{2,1,0:T(8,128)(2,1)} %refs_4_.1, bf16[32,512]{1,0:T(8,128)(2,1)} %bitcast.10, s32[2,128]{1,0:T(2,128)} %bitcast.11, ...), custom_call_target="tpu_custom_call" | custom-call | tf_op jit(solution)/shard_map/whole/pallas_call | solution.py:573
  106.2 1.7 %slice_bitcast_fusion = (bf16[128,512]{1,0:T(8,128)(2,1)}, bf16[128,512]{1,0:T(8,128)(2,1)}) fusion(bf16[2,128,512]{2,1,0:T(8,128)(2,1)} %whole.1), kind=kLoop, calls=%fused_computation | loop fusion | bytes 524288 | tf_op jit(solution)/shard_map/squeeze | solution.py:640

commit v6 on v5

--- a/solution.py
+++ b/solution.py
@@ -506,16 +506,24 @@
                     remote(done.at[k, j], back.at[dp], ret_send, ret_recv, (origin, mp)).start()
             else:
                 remote(done.at[k, j], back.at[dp], ret_send, ret_recv, (origin, mp)).start()
+
+    def settle(k, carry):
         for kind in range(3):
             slot_copy(kind, k).wait_send()
             inner_copy(kind, k).wait_send()
         for kind in range(2):
             cross_copy(kind, k).wait_send()
+        return carry
 
     stages = (
         arrive, functools.partial(forward, slot_copy), first_product, activate,
         functools.partial(forward, inner_copy), second_product, finish,
     )
+
+    for drain in drains:
+        drain()
+    for kind in range(11):
+        gather_copy(kind).wait_send()
 
     def step(i, carry):
         for lag, stage in zip(LAGS, stages):
@@ -526,10 +534,7 @@
 
     lax.fori_loop(0, CHUNKS + LAGS[-1], step, 0)
 
-    for drain in drains:
-        drain()
-    for kind in range(11):
-        gather_copy(kind).wait_send()
+    lax.fori_loop(0, CHUNKS, settle, 0)
     for piece in range(8):
         in_copy(piece).wait_send()
     for kind in range(3):

time: 108 us -> 108 us (level)
  no operation moved by 1% of the time
where the time goes in v6:
time: 108 us
  Pallas kernels  105 us (97%)
  local copies, waits for them, and re-layouts  1.68 us (2%)
  between operations  1.29 us (1%)
    pallas_call x1, Pallas kernels, call(): pl.pallas_call(kernel, out_shape=jax.ShapeDtypeStruct((2, ROWS, SLICE), B...  105 us

profile of v6, /device:TPU:1, one launch (start us, length us, event | category | flops | bytes accessed | tf_op | source)
XLA Modules:
  0.0 107.9 jit_solution(4767794294729119432)
XLA Ops:
  1.3 104.9 %whole.1 = bf16[2,128,512]{2,1,0:T(8,128)(2,1)} custom-call(bf16[128,256]{1,0:T(8,128)(2,1)} %refs_0_.1, bf16[256,4096]{1,0:T(8,128)(2,1)} %refs_1_.1, bf16[128,512]{1,0:T(8,128)(2,1)} %refs_2_.1, bf16[512]{0:T(512)(128)(2,1)} %refs_3_.1, bf16[2,4096,256]{2,1,0:T(8,128)(2,1)} %refs_4_.1, bf16[32,512]{1,0:T(8,128)(2,1)} %bitcast.10, s32[2,128]{1,0:T(2,128)} %bitcast.11, ...), custom_call_target="tpu_custom_call" | custom-call | tf_op jit(solution)/shard_map/whole/pallas_call | solution.py:578
  106.2 1.7 %slice_bitcast_fusion = (bf16[128,512]{1,0:T(8,128)(2,1)}, bf16[128,512]{1,0:T(8,128)(2,1)}) fusion(bf16[2,128,512]{2,1,0:T(8,128)(2,1)} %whole.1), kind=kLoop, calls=%fused_computation | loop fusion | bytes 524288 | tf_op jit(solution)/shard_map/squeeze | solution.py:645
